TPU v7x, 512 devices: a whole 4x4x16 slice. The times are simulated.
512 devices in a mesh: patch: 32 (over y_lo, z), tensor: 16 (over y_hi, x, core).
Axes of the slice: x: 4, y: 4 (y_hi: 2, y_lo: 2; y = y_hi * 2 + y_lo), z: 16, core: 2. Of those that a mesh axis runs over, the one named last changes fastest.
Arguments:
- inputs: bfloat16 [24576, 1024], P('patch'), may hold values from -22.5 to 22.5
- cotangent: bfloat16 [24576, 1024], P('patch'), may hold values from -6 to 6
- norm_gain: float32 [1024], replicated, may hold values from 0.5 to 1.5
- proj_weight: bfloat16 [1024, 4, 1024], P(None, None, 'tensor'), may hold values from -2 to 2
- weight_noise: bfloat16 [1024, 4, 1024], P(None, None, 'tensor'), may hold values from -0.09375 to 0.09375
- patch_counts: int32 [32], replicated, may hold values from 1 to 12, as said below
- neighbours: int32 [384, 9], P('patch'), may hold values from -1 to 35, as said below
- pixel_valid: int32 [384, 64], replicated, may hold values from 0 to 1, as said below
Outputs:
- input_grad: bfloat16 [24576, 1024], P('patch', 'tensor')
- proj_grads: float32 [1024, 4, 1024], P('patch', None, 'tensor')
Inputs may be any that keep to these rules, and one draw needn't show every extreme that they name: `patch_counts`: some device other than the first holds exactly 12 patches. `neighbours`: each row lists the slot itself first, then up to 8 other distinct slots, -1 marking an absent entry; entries index the 36 slots of the previous, own and next device and name only slots below that device's count; a slot at or above its device's count lists only itself. `pixel_valid`: every patch has a valid pixel.
All inputs are finite; a program needn't handle non-finite values.
Results may differ from a plain program's by a relative error of at most 0.03.
The roundings to bfloat16 on the way count: a program that leaves them out, or rounds other values in their place, can miss the bound.
Values may be sent and summed in bfloat16 or wider, within the bound.
A program may use at most 64 MiB of HBM per device.

v0:
```python
import jax
import jax.numpy as jnp
from jax import lax
from jax.sharding import PartitionSpec as P


def extended(cells, sides, width):
    for axis, dim in sides:
        count = lax.axis_size(axis)
        ends = count - 1
        head = lax.slice_in_dim(cells, 0, width, axis=dim)
        tail = lax.slice_in_dim(cells, cells.shape[dim] - width, cells.shape[dim], axis=dim)
        cells = jnp.concatenate(
            [
                lax.ppermute(tail, axis, [(i, (i + 1) % count) for i in range(ends)]),
                cells,
                lax.ppermute(head, axis, [((i + 1) % count, i) for i in range(ends)]),
            ],
            axis=dim,
        )
    return cells


def shifted(value, axis, by):
    devices = lax.axis_size(axis)
    pairs = [(i, i + by) for i in range(devices) if 0 <= i + by < devices]
    return lax.ppermute(value, axis, pairs)


def rms_parts(inputs, norm_gain):
    values = inputs.astype(jnp.float32)
    inverse_rms = lax.rsqrt(jnp.mean(values * values, axis=1, keepdims=True) + 1e-06)
    normed = values * inverse_rms
    hidden = (normed * norm_gain).astype(jnp.bfloat16)
    return (inverse_rms, normed, hidden)


def per_device(
    inputs, cotangent, norm_gain, proj_weight, weight_noise, patch_counts, neighbours, pixel_valid
):
    row_count, width = inputs.shape
    slot_count, nb_count = neighbours.shape
    pixels = row_count // slot_count
    head_size = proj_weight.shape[2]
    factor = head_size ** (-0.5)
    my_index = lax.axis_index("patch")
    my_count = patch_counts[my_index]
    live_rows = jnp.repeat(jnp.arange(slot_count) < my_count, pixels)
    upstream = jnp.where(live_rows[:, None], cotangent, jnp.zeros_like(cotangent))
    inverse_rms, normed, hidden = rms_parts(inputs, norm_gain)
    weights = (proj_weight.astype(jnp.float32) + weight_noise.astype(jnp.float32)).astype(
        jnp.bfloat16
    )
    in_weights = weights[:, :3].reshape(width, 3 * head_size)
    projected = jnp.dot(hidden, in_weights, preferred_element_type=jnp.float32).astype(jnp.bfloat16)
    queries = projected[:, :head_size].reshape(slot_count, pixels, head_size)
    window = extended(projected[:, head_size:], (("patch", 0),), row_count)
    present = neighbours >= 0
    slot_index = jnp.maximum(neighbours, 0)
    padded_valid = jnp.pad(pixel_valid, ((slot_count, slot_count), (0, 0)))
    window_valid = lax.dynamic_slice_in_dim(padded_valid, my_index * slot_count, 3 * slot_count, 0)
    key_valid = ((window_valid[slot_index] > 0) & present[:, :, None]).reshape(
        slot_count, nb_count * pixels
    )
    near = window.reshape(3 * slot_count, pixels, 2 * head_size)[slot_index]
    near = near.reshape(slot_count, nb_count * pixels, 2 * head_size)
    near_keys = near[:, :, :head_size]
    near_values = near[:, :, head_size:]
    scores = (
        jnp.einsum("spd,skd->spk", queries, near_keys, preferred_element_type=jnp.float32) * factor
    )
    scores = jnp.where(key_valid[:, None, :], scores, -jnp.inf)
    row_max = jnp.max(scores, axis=2, keepdims=True)
    exponent = jnp.exp(scores - row_max)
    attention = exponent / jnp.sum(exponent, axis=2, keepdims=True)
    attention_bf = attention.astype(jnp.bfloat16)
    attended = jnp.einsum(
        "spk,skd->spd", attention_bf, near_values, preferred_element_type=jnp.float32
    )
    attended = attended.astype(jnp.bfloat16).reshape(row_count, head_size)
    out_grad = jnp.dot(upstream, weights[:, 3], preferred_element_type=jnp.float32).astype(
        jnp.bfloat16
    )
    out_grad3 = out_grad.reshape(slot_count, pixels, head_size)
    prob_grad = jnp.einsum(
        "spd,skd->spk", out_grad3, near_values, preferred_element_type=jnp.float32
    )
    value_near = jnp.einsum(
        "spk,spd->skd", attention_bf, out_grad3, preferred_element_type=jnp.float32
    )
    score_grad = (
        attention * (prob_grad - jnp.sum(attention * prob_grad, axis=2, keepdims=True)) * factor
    )
    score_grad = score_grad.astype(jnp.bfloat16)
    query_grad = jnp.einsum(
        "spk,skd->spd", score_grad, near_keys, preferred_element_type=jnp.float32
    )
    query_grad = query_grad.astype(jnp.bfloat16).reshape(row_count, head_size)
    key_near = jnp.einsum("spk,spd->skd", score_grad, queries, preferred_element_type=jnp.float32)
    near_grad = jnp.concatenate([key_near, value_near], axis=2)
    near_grad = near_grad.reshape(slot_count * nb_count, pixels * 2 * head_size)
    selector = (
        slot_index.reshape(-1)[:, None] == jnp.arange(3 * slot_count)[None, :]
    ) & present.reshape(-1)[:, None]
    window_grad = jnp.einsum(
        "ew,ef->wf", selector.astype(jnp.float32), near_grad, precision=lax.Precision.HIGHEST
    )
    window_grad = window_grad.reshape(3 * row_count, 2 * head_size)
    from_next = shifted(window_grad[:row_count].astype(jnp.bfloat16), "patch", -1).astype(
        jnp.float32
    )
    from_prev = shifted(window_grad[2 * row_count :].astype(jnp.bfloat16), "patch", 1).astype(
        jnp.float32
    )
    key_value_grad = (window_grad[row_count : 2 * row_count] + from_next + from_prev).astype(
        jnp.bfloat16
    )
    grads = jnp.concatenate([query_grad, key_value_grad], axis=1)
    feature_part = lax.dot_general(
        grads, in_weights, (((1,), (1,)), ((), ())), preferred_element_type=jnp.float32
    )
    share = width // lax.axis_size("tensor")
    tensor_index = lax.axis_index("tensor")
    feature_grad = lax.psum(feature_part.astype(jnp.bfloat16), "tensor").astype(jnp.float32)
    scaled = feature_grad * norm_gain
    mean_term = jnp.sum(scaled * normed, axis=1, keepdims=True) / width
    full_grad = inverse_rms * (scaled - normed * mean_term)
    local_grad = lax.dynamic_slice_in_dim(full_grad, tensor_index * share, share, 1)
    upstream_share = lax.dynamic_slice_in_dim(upstream, tensor_index * share, share, 1).astype(
        jnp.float32
    )
    input_grad = (upstream_share + local_grad).astype(jnp.bfloat16)
    in_term = lax.dot_general(
        hidden, grads, (((0,), (0,)), ((), ())), preferred_element_type=jnp.float32
    )
    out_term = lax.dot_general(
        upstream, attended, (((0,), (0,)), ((), ())), preferred_element_type=jnp.float32
    )
    proj_grads = lax.psum_scatter(
        jnp.concatenate(
            [
                in_term.reshape(
                    lax.axis_size("patch") * (width // lax.axis_size("patch")), 3, head_size
                ),
                out_term[:, None, :],
            ],
            axis=1,
        ).astype(jnp.bfloat16),
        "patch",
        scatter_dimension=0,
        tiled=True,
    ).astype(jnp.float32)
    return (input_grad, proj_grads)


def solution(mesh):
    placed = (
        P("patch", None),
        P("patch", None),
        P(),
        P(None, None, "tensor"),
        P(None, None, "tensor"),
        P(),
        P("patch", None),
        P(),
    )
    return jax.shard_map(
        per_device,
        mesh=mesh,
        in_specs=placed,
        out_specs=(P("patch", "tensor"), P("patch", None, "tensor")),
        check_vma=False,
    )
```

profile of v0, /device:TPU:1, one launch (start us, length us, event | category | flops | bytes accessed | tf_op | source)
XLA Modules:
  0.0 525.1 jit_solution(10604357023752812487)
XLA Ops:
  7.2 0.0 copy-start.1
  7.2 0.0 all-reduce.7.cloned.1.call-start
  7.2 1.9 fusion.2
  9.1 1.4 add_convert_fusion
  10.6 0.0 copy-start.9
  10.6 0.0 copy-start.11
  10.6 0.0 copy-start.8
  10.6 0.8 convolution_convert_fusion.2
  11.4 1.3 collective-permute-start.1
  12.7 5.0 collective-permute-start
  17.8 0.6 dynamic_slice.12
  18.4 0.6 iota_compare_fusion.1
  19.1 0.1 broadcast_in_dim.45
  19.1 0.1 broadcast_in_dim.46
  19.2 0.1 and.30
  19.3 0.1 reshape.84
  19.4 0.1 copy.30
  19.6 0.6 gather_fusion
  20.3 0.1 broadcast_and_fusion
  20.4 0.1 and.29
  20.5 0.9 reshape.74
  21.3 1.6 broadcast_select_fusion
  22.9 0.6 convolution_convert_fusion.4
  23.5 0.9 reshape.77
  24.4 0.0 collective-permute-done.1
  24.4 0.0 collective-permute-done
  24.5 0.3 copy.31
  24.8 2.0 gather_fusion.1
  26.8 4.0 fusion.13
  30.9 3.1 fusion.70
  34.0 2.6 fusion.25
  36.5 1.8 fusion.35
  38.3 0.4 fusion.28
  38.8 1.1 copy.40
  39.8 9.0 %fusion.8 = f32[12,576,64]{1,2,0:T(8,128)} fusion(f32[12,64,576]{2,1,0:T(8,128)} %fusion.13, bf16[12,64,64]{1,0,2:T(8,128)(2,1)} %reshape.74, f32[12,64,576]{2,1,0:T(8,128)} %get-tuple-element.14, f32[12,64]{1,0:T(8,128)S(1)} %get-tuple-element.13), kind=kOutput, calls=%fused_computation.18 | convolution fusion | flops 59721024 | bytes 5409792 | tf_op jit(solution)/shard_map/spk,spd->skd/dot_general | solution.py:99
  48.8 4.3 pad_maximum_fusion
  53.1 5.3 %copy.38 = f32[12,576,128]{2,1,0:T(8,128)} copy(f32[12,576,128]{1,2,0:T(8,128)} %pad_maximum_fusion) | data formatting | bytes 7077888 | tf_op jit(solution)/shard_map/concatenate | solution.py:100
  58.4 4.8 reshape.79
  63.2 4.6 fusion.75
  67.9 0.8 fusion.69
  68.7 1.1 convert_element_type.78
  69.8 1.8 convert_element_type.80
  71.6 4.2 collective-permute-start.3
  75.8 1.5 collective-permute-start.2
  77.3 2.0 slice.54
  79.3 1.9 slice.41
  81.1 8.2 %fusion.20 = bf16[12,64,64]{2,1,0:T(8,128)(2,1)} fusion(bf16[12,576,128]{2,1,0:T(8,128)(2,1)S(1)} %bitcast.27, f32[12,64,576]{2,1,0:T(8,128)} %fusion.13, f32[12,64,576]{2,1,0:T(8,128)} %get-tuple-element.14, f32[12,64]{1,0:T(8,128)S(1)} %get-tuple-element.13), kind=kOutput, calls=%fused_computation.30 | convolution fusion | flops 59770176 | bytes 9748480 | tf_op jit(solution)/shard_map/spk,skd->spd/dot_general | solution.py:95
  89.3 0.0 collective-permute-done.3
  89.3 1.2 add_convert_fusion.1
  90.6 2.4 convolution_convert_fusion.1
  93.0 0.7 copy.39
  93.8 2.3 pad_maximum_fusion.1
  96.1 0.0 all-reduce.7.cloned.1.call-update
  96.1 0.0 copy-start.2
  96.1 0.0 all-reduce.5.cloned.1.call-start
  96.2 2.9 convolution_convert_fusion
  99.1 0.0 all-reduce.5.cloned.1.call-update
  99.1 1.3 dynamic-slice
  101.0 238.6 %all-reduce.7.cloned.1.call-done = bf16[1024,4,64]{2,1,0:T(4,128)(2,1)} async-done(((bf16[1024,4,64]{2,1,0:T(4,128)(2,1)}), bf16[1024,4,64]{2,1,0:T(4,128)(2,1)}) %all-reduce.7.cloned.1.call-update) | async-done | bytes 524304
  339.6 1.4 dynamic-slice_convert_fusion
  341.0 173.8 %all-reduce.5.cloned.1.call-done = bf16[768,1024]{1,0:T(8,128)(2,1)} async-done(((bf16[768,1024]{1,0:T(8,128)(2,1)}), bf16[768,1024]{1,0:T(8,128)(2,1)}) %all-reduce.5.cloned.1.call-update) | async-done | bytes 1572880 | tf_op jit(solution)/shard_map/psum | solution.py:124
  514.8 2.2 multiply_reduce_fusion
  517.0 0.5 fusion.39
  517.5 0.8 copy.41
  (34 shorter events, 0.2 us)
Async XLA Ops:
  7.2 3.4 copy-start.1
  7.2 3.4 copy-start.10
  7.2 332.4 %all-reduce.7.cloned.1.call-start = ((), (), s32[]{:S(2)}) async-start(), calls=%async_computation.1 | async-start | bytes 2097152
  10.6 0.9 copy-start.4
  10.6 7.2 %copy-start.9 = (s32[12,9]{1,0:T(8,128)S(1)}, s32[12,9]{1,0:T(8,128)}, u32[]{:S(2)}) copy-start(s32[12,9]{1,0:T(8,128)} %param.14) | copy-start | bytes 1300
  10.6 7.2 %copy-start.11 = (s32[32]{0:T(128)S(1)}, s32[32]{0:T(128)}, u32[]{:S(2)}) copy-start(s32[32]{0:T(128)} %param.13) | copy-start | bytes 388
  10.6 8.8 %copy-start.8 = (s32[384,64]{0,1:T(8,128)S(1)}, s32[384,64]{0,1:T(8,128)}, u32[]{:S(2)}) copy-start(s32[384,64]{0,1:T(8,128)} %param.15) | copy-start | bytes 294916
  11.4 13.0 %collective-permute-start.1 = (bf16[768,128]{0,1:T(8,128)(2,1)S(1)}, bf16[768,128]{0,1:T(8,128)(2,1)S(1)}, u32[]{:S(2)}, u32[]{:S(2)}) collective-permute-start(bf16[768,128]{0,1:T(8,128)(2,1)S(1)} %slice.50), channel_id=1, source_target_pairs={{16,0},{32,16},{48,32},{64,48},{80,64},{96,80},{112,96},{128,112},... | collective-permute-start | bytes 589832 | tf_op jit(solution)/shard_map/ppermute | solution.py:17
  12.7 11.7 %collective-permute-start = (bf16[768,128]{0,1:T(8,128)(2,1)S(1)}, bf16[768,128]{0,1:T(8,128)(2,1)S(1)}, u32[]{:S(2)}, u32[]{:S(2)}) collective-permute-start(bf16[768,128]{0,1:T(8,128)(2,1)S(1)} %slice.50), channel_id=1, source_target_pairs={{0,16},{16,32},{32,48},{48,64},{64,80},{80,96},{96,112},{112,128},... | collective-permute-start | bytes 589832 | tf_op jit(solution)/shard_map/ppermute | solution.py:15
  26.8 4.0 copy-start
  34.0 2.6 copy-start.6
  34.0 2.6 copy-start.12
  71.6 17.7 %collective-permute-start.3 = (bf16[768,128]{1,0:T(8,128)(2,1)}, bf16[768,128]{1,0:T(8,128)(2,1)}, u32[]{:S(2)}, u32[]{:S(2)}) collective-permute-start(bf16[768,128]{1,0:T(8,128)(2,1)} %convert_element_type.80), channel_id=1, source_target_pairs={{0,16},{16,32},{32,48},{48,64},{64,80},{80,96},{96,112},{112,128},... | collective-permute-start | bytes 589832 | tf_op jit(solution)/shard_map/ppermute | solution.py:27
  75.8 13.5 %collective-permute-start.2 = (bf16[768,128]{1,0:T(8,128)(2,1)S(1)}, bf16[768,128]{1,0:T(8,128)(2,1)}, u32[]{:S(2)}, u32[]{:S(2)}) collective-permute-start(bf16[768,128]{1,0:T(8,128)(2,1)S(1)} %convert_element_type.78), channel_id=1, source_target_pairs={{16,0},{32,16},{48,32},{64,48},{80,64},{96,80},{112,96},{128,112},... | collective-permute-start | bytes 589832 | tf_op jit(solution)/shard_map/ppermute | solution.py:27
  90.5 2.5 copy-start.7
  90.6 3.2 copy-start.3
  93.7 2.4 copy-start.5
  96.1 418.7 %copy-start.2 = (bf16[768,1024]{1,0:T(8,128)(2,1)S(1)}, bf16[768,1024]{1,0:T(8,128)(2,1)}, u32[]{:S(2)}) copy-start(bf16[768,1024]{1,0:T(8,128)(2,1)} %param.8) | copy-start | bytes 4718596
  96.1 418.7 %all-reduce.5.cloned.1.call-start = ((), (), s32[]{:S(2)}) async-start(), calls=%async_computation | async-start | bytes 3145728 | tf_op jit(solution)/shard_map/psum | solution.py:124
Sparse Core Ops, SparseCore 0:
  96.2 243.3 all-reduce.6
  342.8 171.9 all-reduce.4
where the time goes:
time: 526 us; the launch traced here: 525 us
  waiting for transfers between devices  412 us (78%)
  matrix products  40.4 us (8%)
  local copies, waits for them, and re-layouts  27.6 us (5%)
  other arithmetic  17.6 us (3%)
  between operations  15.1 us (3%)
  starting transfers between devices  12.1 us (2%)
    unnamed x3, waiting for transfers between devices  239 us
    psum x1, waiting for transfers between devices, per_device(): lax.psum(feature_part.astype(jnp.bfloat16), 'tensor').astype(jnp.float32)  174 us
  transfers between devices with their start and end apart: 6, of which 2 were waited for; matrix products, arithmetic and copies ran while one was open for 5% of the time, Pallas kernels for 0%

commit v1 on v0

v1 whole, which is shorter than its diff:
```python
import jax
import jax.numpy as jnp
from jax import lax
from jax.experimental import pallas as pl
from jax.experimental.pallas import tpu as pltpu
from jax.sharding import PartitionSpec as P

BF = jnp.bfloat16
F32 = jnp.float32
MESH = pl.DeviceIdType.MESH
OFF = -1e30

ROWS = 768
D = 1024
PIX = 64
CAP = 12
NB = 9
TILE = 256
Z = 16
NX = 4


def nn(a, b):
    return lax.dot_general(a, b, (((1,), (0,)), ((), ())), preferred_element_type=F32)


def nt(a, b):
    return lax.dot_general(a, b, (((1,), (1,)), ((), ())), preferred_element_type=F32)


def tile(i, size=TILE):
    if isinstance(i, int):
        return pl.ds(i * size, size)
    return pl.ds(pl.multiple_of(i * size, size), size)


def remote(src, dst, send_sem, recv_sem, **device):
    return pltpu.make_async_remote_copy(
        src_ref=src,
        dst_ref=dst,
        send_sem=send_sem,
        recv_sem=recv_sem,
        device_id=device,
        device_id_type=MESH,
    )


def kernel(
    x_ref, g_ref, gain_ref, w_ref, counts_ref, nb_ref, pv_ref,
    og_ref, pg_ref,
    hid, up, irms, nshare, ushare, kvw, kvt, kaug, qaug, qz, dz, q_t,
    sc, dp, mx, pt, ds_t, halo_out, own_grad, halo_in, att_t, grads_t,
    m_out, m_in, pj, y_in, z_out, z_in,
    part, r1, s2, r2, r3, s3, r4,
    halo_s, halo_r, hg_s, hg_r, m_s, m_r, y_s, y_r, z_s, z_r,
    c_s, c_r, r2_s, r2_r, r3_s, r3_r, r4_s, r4_r,
):
    p = lax.axis_index("patch")
    t = lax.axis_index("tensor")
    y_lo, z = p // Z, p % Z
    core = t % 2
    x = (t // 2) % NX
    y_hi = t // 8
    right, left = (p + 1) % 32, (p + 31) % 32
    y_partner = (1 - y_lo) * Z + z
    row0 = t - x * 2
    x_right, x_left = row0 + ((x + 1) % NX) * 2, row0 + ((x + 3) % NX) * 2
    core_partner = t + 1 - 2 * core
    hi_partner = (t + 8) % 16

    def z_peer(r):
        return y_lo * Z + (z + r) % Z

    barrier = pltpu.get_barrier_semaphore()

    def greet(r, carry):
        pl.semaphore_signal(barrier, inc=1, device_id={"patch": z_peer(r)}, device_id_type=MESH)
        pl.semaphore_signal(barrier, inc=1, device_id={"tensor": (t + r) % 16}, device_id_type=MESH)
        return carry

    lax.fori_loop(1, 16, greet, 0)
    for other in (left, right, y_partner):
        pl.semaphore_signal(barrier, inc=1, device_id={"patch": other}, device_id_type=MESH)

    gain = gain_ref[...]

    def project(i, carry):
        rows = tile(i)
        xs = x_ref[rows, :].astype(F32)
        inv = lax.rsqrt(jnp.sum(xs * xs, axis=1, keepdims=True) * (1.0 / D) + 1e-06)
        h = (xs * inv * gain).astype(BF)
        hid[rows, :] = h
        irms[rows, :] = jnp.broadcast_to(inv, (TILE, 128))
        pr = nn(h, w_ref[...])
        kvw[1, rows, :] = pr[:, :128].astype(BF)
        lane = lax.broadcasted_iota(jnp.int32, (TILE, 128), 1)
        q = jnp.where(lane < 64, pr[:, 128:].astype(BF).astype(F32), 0.0)
        qz[rows, :] = (q * 0.125).astype(BF)
        q_t[:, rows] = jnp.transpose(q)[:64, :].astype(BF)
        return carry

    lax.fori_loop(0, 3, project, 0)

    pl.semaphore_wait(barrier, 33)
    to_next = remote(kvw.at[1], kvw.at[0], halo_s.at[0], halo_r.at[0], patch=right)
    to_prev = remote(kvw.at[1], kvw.at[2], halo_s.at[1], halo_r.at[1], patch=left)
    to_next.start()
    to_prev.start()

    lane12 = lax.broadcasted_iota(jnp.int32, (CAP, 128), 1)
    nb = nb_ref[...]
    member = lane12 == 64 + nb[:, 0:1]
    for j in range(1, NB):
        member = member | (lane12 == 64 + nb[:, j : j + 1])
    member = jnp.where(member, 0.0, OFF)
    member = jnp.where(lane12 == 100, 1.0, jnp.where(lane12 > 100, 0.0, member))
    lane64 = lax.broadcasted_iota(jnp.int32, (PIX, 128), 1)
    row64 = lax.broadcasted_iota(jnp.int32, (PIX, PIX), 0)
    col64 = lax.broadcasted_iota(jnp.int32, (PIX, PIX), 1)
    for b, owner in enumerate((left, p, right)):
        valid = jnp.where(pv_ref[pl.ds(owner * CAP, CAP), :] > 0, 0.0, OFF)
        for s in range(CAP):
            off = jnp.sum(
                jnp.where(row64 == col64, valid[s : s + 1, :], 0.0), axis=1, keepdims=True
            )
            aux = jnp.where(lane64 == 64 + b * CAP + s, 1.0, 0.0)
            aux = jnp.where(lane64 == 100, off, aux)
            kaug[b, s * PIX : (s + 1) * PIX, :] = aux.astype(BF)

    live = counts_ref[p] * PIX

    def upstream(i, carry):
        rows = tile(i)
        row = lax.broadcasted_iota(jnp.int32, (TILE, 1), 0) + i * TILE
        g = jnp.where(row < live, g_ref[rows, :].astype(F32), 0.0).astype(BF)
        up[rows, :] = g
        og = nn(g, w_ref[:, 128:])
        lane = lax.broadcasted_iota(jnp.int32, (TILE, 128), 1)
        dz[rows, :] = jnp.where(lane >= 64, og, 0.0).astype(BF)
        return carry

    lax.fori_loop(0, 3, upstream, 0)
    for s in range(CAP):
        rows = slice(s * PIX, (s + 1) * PIX)
        qaug[rows, :] = jnp.where(lane64 < 64, qz[rows, :].astype(F32), member[s : s + 1, :]).astype(BF)

    mx[...] = jnp.full_like(mx, 2.0 * OFF)

    def score(b):
        def step(i, carry):
            rows = tile(i)
            lane = lax.broadcasted_iota(jnp.int32, (TILE, 128), 1)
            kv = kvw[b, rows, :]
            ka = jnp.where(lane < 64, kv.astype(F32), kaug[b, rows, :].astype(F32)).astype(BF)
            kvt[b, :, rows] = jnp.transpose(kv.astype(F32)).astype(BF)
            at = tile(b * 3 + i)
            for q in range(3):
                cols = tile(q)
                s = nt(ka, qaug[cols, :])
                sc[at, cols] = s
                mx[:, cols] = jnp.maximum(mx[:, cols], jnp.max(s.reshape(32, 8, TILE), axis=0))
                dp[at, cols] = nt(kv, dz[cols, :])
            return carry

        lax.fori_loop(0, 3, step, 0)

    score(1)

    odd = core == 1
    share = pl.ds(pl.multiple_of((t // 2) * 128, 128), 128)
    gain_share = gain_ref[:, share]
    gain_share = jnp.where(odd, pltpu.roll(gain_share, 64, 1), gain_share)

    def shares(i, carry):
        rows = tile(i)
        xs = x_ref[rows, share].astype(F32)
        nshare[rows, :] = jnp.where(odd, pltpu.roll(xs, 64, 1), xs) * irms[rows, :]
        us = up[rows, share].astype(F32)
        ushare[rows, :] = jnp.where(odd, pltpu.roll(us, 64, 1), us)
        return carry

    lax.fori_loop(0, 3, shares, 0)

    to_next.wait_recv()
    score(0)
    to_prev.wait_recv()
    score(2)

    def soften(q, carry):
        cols = tile(q)
        top = jnp.max(mx[:, cols], axis=0, keepdims=True)

        def first(i, sums):
            total, weighted = sums
            rows = tile(i)
            e = jnp.exp(sc[rows, cols] - top)
            sc[rows, cols] = e
            total = total + jnp.sum(e.reshape(32, 8, TILE), axis=0)
            weighted = weighted + jnp.sum((e * dp[rows, cols]).reshape(32, 8, TILE), axis=0)
            return total, weighted

        zero = jnp.zeros((8, TILE), F32)
        total, weighted = lax.fori_loop(0, 9, first, (zero, zero))
        inv = 1.0 / jnp.sum(total, axis=0, keepdims=True)
        delta = jnp.sum(weighted, axis=0, keepdims=True) * inv

        def second(i, carry):
            rows = tile(i)
            att = sc[rows, cols] * inv
            pt[rows, cols] = att.astype(BF)
            ds_t[rows, cols] = (att * (dp[rows, cols] - delta)).astype(BF)
            return carry

        lax.fori_loop(0, 9, second, 0)
        return carry

    lax.fori_loop(0, 3, soften, 0)

    def near_grad(b, i):
        at = tile(b * 3 + i)
        return nn(ds_t[at, :], qz[...]) + nn(pt[at, :], dz[...])

    def halo_grad(b, slot):
        def step(i, carry):
            halo_out[slot, tile(i), :] = near_grad(b, i).astype(BF)
            return carry

        lax.fori_loop(0, 3, step, 0)

    halo_grad(0, 0)
    grad_prev = remote(halo_out.at[0], halo_in.at[1], hg_s.at[0], hg_r.at[0], patch=left)
    grad_prev.start()
    halo_grad(2, 1)
    grad_next = remote(halo_out.at[1], halo_in.at[0], hg_s.at[1], hg_r.at[1], patch=right)
    grad_next.start()

    def own(i, carry):
        own_grad[tile(i), :] = near_grad(1, i)
        return carry

    lax.fori_loop(0, 3, own, 0)

    def query_side(q, carry):
        cols = tile(q)
        qg = jnp.zeros((64, TILE), F32)
        at = jnp.zeros((64, TILE), F32)
        for b in range(3):
            rows = slice(b * ROWS, (b + 1) * ROWS)
            qg = qg + nn(kvt[b, 0:64, :], ds_t[rows, cols])
            at = at + nn(kvt[b, 64:128, :], pt[rows, cols])
        grads_t[128:192, cols] = (qg * 0.125).astype(BF)
        att_t[:, cols] = at.astype(BF)
        return carry

    lax.fori_loop(0, 3, query_side, 0)

    def weight_qo(n, carry):
        cols = tile(n)
        both = jnp.concatenate(
            [nn(grads_t[128:192, :], hid[:, cols]), nn(att_t[...], up[:, cols])], axis=0
        )
        pj[0, cols, :] = jnp.transpose(both).astype(BF)
        return carry

    lax.fori_loop(0, 4, weight_qo, 0)

    def y_copy(h):
        return remote(
            pj.at[h, tile(1 - y_lo, 512), :], y_in.at[h], y_s.at[h], y_r.at[h], patch=y_partner
        )

    y_copy(0).start()

    grad_next.wait_recv()
    grad_prev.wait_recv()

    def collect(i, carry):
        rows = tile(i)
        total = (
            own_grad[rows, :] + halo_in[0, rows, :].astype(F32) + halo_in[1, rows, :].astype(F32)
        )
        kvg = jnp.transpose(total).astype(BF)
        grads_t[0:128, rows] = kvg
        prod = jnp.sum(kvg.astype(F32) * kvt[1, :, rows].astype(F32), axis=0, keepdims=True)
        qg = grads_t[128:192, rows].astype(F32) * q_t[:, rows].astype(F32)
        prod = prod + jnp.sum(qg, axis=0, keepdims=True)
        for j in range(2):
            m_out[pl.ds(2 * i + j, 1), :] = prod[:, j * 128 : (j + 1) * 128]
        return carry

    m_out[...] = jnp.zeros_like(m_out)
    lax.fori_loop(0, 3, collect, 0)

    def m_send(r, carry):
        remote(m_out, m_in.at[r - 1], m_s, m_r, tensor=(t + r) % 16).start()
        return carry

    lax.fori_loop(1, 16, m_send, 0)

    order = [(2, 0), (2, 1), (1, 0), (3, 0), (0, 0), (1, 1), (3, 1), (0, 1)]

    def block_of(o):
        dx, k = order[o]
        y = (1 - y_hi) if k == 0 else y_hi
        return y * NX + (x + dx) % NX

    def core_copy(o):
        return remote(
            part.at[o, tile(1 - core, 64), :], r1.at[o], c_s.at[o], c_r.at[o], tensor=core_partner
        )

    for o in range(8):
        rows = tile(block_of(o), 128)
        part[o] = nn(w_ref[rows, 0:192], grads_t[...]).astype(BF)
        core_copy(o).start()

    def weight_kv(n, carry):
        cols = tile(n)
        pj[1, cols, :] = jnp.transpose(nn(grads_t[0:128, :], hid[:, cols])).astype(BF)
        return carry

    lax.fori_loop(0, 4, weight_kv, 0)
    y_copy(1).start()

    def pair_sum(o):
        core_copy(o).wait_recv()
        return part[o, tile(core, 64), :].astype(F32) + r1[o].astype(F32)

    def r2_copy(k, side):
        half = slice(side * 32, side * 32 + 32)
        return remote(
            s2.at[k, half, :], r2.at[side, k], r2_s.at[side, k], r2_r.at[side, k],
            tensor=x_right if side == 0 else x_left,
        )

    def r3_copy(k, side, half):
        o = 2 + 3 * k + side
        rows = slice(half * 32, half * 32 + 32)
        return remote(
            s2.at[o, rows, :], r3.at[side, k, rows, :], r3_s.at[side, k, half], r3_r.at[side, k, half],
            tensor=x_right if side == 0 else x_left,
        )

    def z_copy(h, r):
        return remote(
            z_out.at[h, tile((z + r) % Z, 32), :], z_in.at[h, r - 1], z_s.at[h], z_r.at[h],
            patch=z_peer(r),
        )

    def z_stage(h):
        y_copy(h).wait_recv()
        z_out[h] = (
            pj[h, tile(y_lo, 512), :].astype(F32) + y_in[h].astype(F32)
        ).astype(BF)

        def step(r, carry):
            z_copy(h, r).start()
            return carry

        lax.fori_loop(1, Z, step, 0)

    for k in range(2):
        s2[k] = pair_sum(k).astype(BF)
        for side in range(2):
            r2_copy(k, side).start()
    for k in range(2):
        for side in range(2):
            o = 2 + 3 * k + side
            s2[o] = pair_sum(o).astype(BF)
            r3_copy(k, side, 1 - side).start()
    z_stage(0)
    for k in range(2):
        for side in range(2):
            o = 2 + 3 * k + side
            half = slice(side * 32, side * 32 + 32)
            r2_copy(k, side).wait_recv()
            s2[o, half, :] = (
                pair_sum_again(part, r1, core, o, half) + r2[side, k].astype(F32)
            ).astype(BF)
            r3_copy(k, side, side).start()
    z_stage(1)

    def x_sum(k):
        o = 4 + 3 * k
        total = pair_sum(o)
        for side in range(2):
            for half in range(2):
                r3_copy(k, side, half).wait_recv()
            total = total + r3[side, k].astype(F32)
        return total

    r4_copy = remote(s3, r4, r4_s, r4_r, tensor=hi_partner)
    s3[...] = x_sum(0).astype(BF)
    r4_copy.start()
    feature = x_sum(1)

    for h in range(2):
        pltpu.make_async_copy(z_in.at[h], z_in.at[h], z_r.at[h]).wait()
        total = z_out[h, tile(z, 32), :].astype(F32)
        for r in range(Z - 1):
            total = total + z_in[h, r].astype(F32)
        pg_ref[h] = total

    pltpu.make_async_copy(m_in, m_in, m_r).wait()
    m = m_out[...]
    for r in range(15):
        m = m + m_in[r]
    m = m * (1.0 / D)
    mean = jnp.concatenate([m[i : i + 1, :] for i in range(6)], axis=1)

    r4_copy.wait_recv()
    feature = feature + r4[...].astype(F32)
    both = jnp.concatenate([feature, jnp.broadcast_to(mean, (64, ROWS))], axis=0)
    for i in range(3):
        rows = slice(i * TILE, (i + 1) * TILE)
        turned = jnp.transpose(both[:, rows])
        means = pltpu.roll(turned, 64, 1)
        grad = ushare[rows, :] + irms[rows, :] * (turned * gain_share - nshare[rows, :] * means)
        og_ref[rows, :] = grad[:, :64].astype(BF)

    to_next.wait_send()
    to_prev.wait_send()
    grad_prev.wait_send()
    grad_next.wait_send()
    for o in range(8):
        core_copy(o).wait_send()
    for k in range(2):
        for side in range(2):
            r2_copy(k, side).wait_send()
            for half in range(2):
                r3_copy(k, side, half).wait_send()
    r4_copy.wait_send()
    for h in range(2):
        y_copy(h).wait_send()
        pltpu.make_async_copy(z_in.at[h], z_in.at[h], z_s.at[h]).wait()
    pltpu.make_async_copy(m_in, m_in, m_s).wait()


def pair_sum_again(part, r1, core, o, half):
    rows = pl.ds(pl.multiple_of(core * 64 + half.start, 32), 32)
    return part[o, rows, :].astype(F32) + r1[o, half, :].astype(F32)


def per_device(
    inputs, cotangent, norm_gain, proj_weight, weight_noise, patch_counts, neighbours, pixel_valid
):
    weights = (proj_weight.astype(F32) + weight_noise.astype(F32)).astype(BF)
    weights = jnp.concatenate(
        [weights[:, 1], weights[:, 2], weights[:, 0], weights[:, 3]], axis=1
    )
    vmem = pl.BlockSpec(memory_space=pltpu.VMEM)
    smem = pl.BlockSpec(memory_space=pltpu.SMEM)
    V = pltpu.VMEM
    dma = pltpu.SemaphoreType.DMA
    grad, proj = pl.pallas_call(
        kernel,
        out_shape=(
            jax.ShapeDtypeStruct((ROWS, 64), BF),
            jax.ShapeDtypeStruct((2, 32, 128), F32),
        ),
        in_specs=[vmem, vmem, vmem, vmem, smem, vmem, vmem],
        out_specs=(vmem, vmem),
        scratch_shapes=[
            V((ROWS, D), BF),
            V((ROWS, D), BF),
            V((ROWS, 128), F32),
            V((ROWS, 128), F32),
            V((ROWS, 128), F32),
            V((3, ROWS, 128), BF),
            V((3, 128, ROWS), BF),
            V((3, ROWS, 128), BF),
            V((ROWS, 128), BF),
            V((ROWS, 128), BF),
            V((ROWS, 128), BF),
            V((64, ROWS), BF),
            V((3 * ROWS, ROWS), F32),
            V((3 * ROWS, ROWS), F32),
            V((8, ROWS), F32),
            V((3 * ROWS, ROWS), BF),
            V((3 * ROWS, ROWS), BF),
            V((2, ROWS, 128), BF),
            V((ROWS, 128), F32),
            V((2, ROWS, 128), BF),
            V((64, ROWS), BF),
            V((192, ROWS), BF),
            V((8, 128), F32),
            V((15, 8, 128), F32),
            V((2, D, 128), BF),
            V((2, 512, 128), BF),
            V((2, 512, 128), BF),
            V((2, 15, 32, 128), BF),
            V((8, 128, ROWS), BF),
            V((8, 64, ROWS), BF),
            V((8, 64, ROWS), BF),
            V((2, 2, 32, ROWS), BF),
            V((2, 2, 64, ROWS), BF),
            V((64, ROWS), BF),
            V((64, ROWS), BF),
            dma((2,)), dma((2,)),
            dma((2,)), dma((2,)),
            dma, dma,
            dma((2,)), dma((2,)),
            dma((2,)), dma((2,)),
            dma((8,)), dma((8,)),
            dma((2, 2)), dma((2, 2)),
            dma((2, 2, 2)), dma((2, 2, 2)),
            dma, dma,
        ],
        compiler_params=pltpu.CompilerParams(
            collective_id=0, has_side_effects=True, vmem_limit_bytes=56 * 1024 * 1024
        ),
        cost_estimate=pl.CostEstimate(
            flops=4 * 10**9, bytes_accessed=5 * 10**6, transcendentals=2 * 10**6
        ),
    )(
        inputs,
        cotangent,
        norm_gain.reshape(1, D),
        weights,
        patch_counts,
        neighbours,
        pixel_valid,
    )
    proj = jnp.stack([proj[0, :, :64], proj[1, :, :64], proj[1, :, 64:], proj[0, :, 64:]], axis=1)
    return (grad, proj)


def solution(mesh):
    placed = (
        P("patch", None),
        P("patch", None),
        P(),
        P(None, None, "tensor"),
        P(None, None, "tensor"),
        P(),
        P("patch", None),
        P(),
    )
    return jax.shard_map(
        per_device,
        mesh=mesh,
        in_specs=placed,
        out_specs=(P("patch", "tensor"), P("patch", None, "tensor")),
        check_vma=False,
    )
```

time: 526 us -> 66.8 us (0.13)
  waiting for transfers between devices: 412 us -> 0 us
  Pallas kernels: 0 us -> 58.2 us
  matrix products: 40.4 us -> 0 us
  local copies, waits for them, and re-layouts: 27.6 us -> 6.17 us
  other arithmetic: 17.6 us -> 1.43 us
  between operations: 15.1 us -> 0.7 us
  starting transfers between devices: 12.1 us -> 0 us
    unnamed x3 -> x0, waiting for transfers between devices: 239 us -> none
    psum x1 -> x0, waiting for transfers between devices: 174 us -> none  [per_device(): lax.psum(feature_part.astype(jnp.bfloat16), 'tensor').astype(jnp.float32)]
    pallas_call x0 -> x1, Pallas kernels: none -> 58.2 us  [per_device(): pl.pallas_call(kernel, out_shape=(jax.ShapeDtypeStruct((ROWS, 64), BF), j...]
    dot_general x11 -> x0, matrix products: 37.3 us -> none  [the longest x1 9 us: per_device(): jnp.einsum('spk,spd->skd', score_grad, queries, preferred_element_type=jn...]
    ppermute x4 -> x0, starting transfers between devices: 12 us -> none  [the longest x2 5.67 us: shifted(): return lax.ppermute(value, axis, pairs)]
    reshape x4 -> x0, local copies, waits for them, and re-layouts: 7.25 us -> none  [the longest x1 4.79 us: per_device(): near_grad = near_grad.reshape(slot_count * nb_count, pixels * 2 * head_size)]
    concatenate x2 -> x0, local copies, waits for them, and re-layouts: 5.62 us -> none  [the longest x1 5.32 us: per_device(): near_grad = jnp.concatenate([key_near, value_near], axis=2)]
    concatenate x3 -> x1, other arithmetic: 6.65 us -> 1.15 us  [per_device(): jnp.concatenate([weights[:, 1], weights[:, 2], weights[:, 0], weights[:,...]
  transfers between devices with their start and end apart: 6 -> 0, of which waited for: 2 -> 0; matrix products, arithmetic and copies ran while one was open for 5% -> 0% of each run, Pallas kernels for 0% -> 0%
where the time goes in v1:
time: 66.8 us; the launch traced here: 66.5 us
  Pallas kernels  58.2 us (87%)
  local copies, waits for them, and re-layouts  6.17 us (9%)
  other arithmetic  1.43 us (2%)
  between operations  0.7 us (1%)
    pallas_call x1, Pallas kernels, per_device(): pl.pallas_call(kernel, out_shape=(jax.ShapeDtypeStruct((ROWS, 64), BF), j...  58.2 us
    unnamed x9, local copies, waits for them, and re-layouts  5.23 us

profile of v1, /device:TPU:1, one launch (start us, length us, event | category | flops | bytes accessed | tf_op | source)
XLA Modules:
  0.0 66.5 jit_solution(14686733627950246632)
XLA Ops:
  0.6 0.0 copy-start
  0.6 1.6 %copy.10 = bf16[1024,4,64]{2,0,1:T(8,128)(2,1)S(1)} copy(bf16[1024,4,64]{0,2,1:T(8,128)(2,1)} %param.11) | data formatting | bytes 1048576 | tf_op args[3]
  2.2 0.0 copy-done
  2.2 0.5 copy.11
  2.7 0.3 add_convert_fusion
  3.0 0.0 copy-start.1
  3.0 0.1 slice_bitcast_fusion.3
  3.1 1.1 %pad_maximum_fusion.w_ref = bf16[1024,256]{1,0:T(8,128)(2,1)} fusion(bf16[1024,64]{1,0:T(8,128)(2,1)S(1)} %get-tuple-element.9, bf16[1024,64]{1,0:T(8,128)(2,1)S(1)} %get-tuple-element.10, bf16[1024,64]{1,0:T(8,128)(2,1)S(1)} %get-tuple-element.11, bf16[1024,64]{1,0:T(8,128)(2,1)S(1)} %get-tuple-element.8), kind=kLoop, calls=%fused_computation.1 | loop fusion | flops 2097152 | bytes 1048576 | tf_op jit(solution)/shard_map/concatenate | solution.py:448
  4.2 0.0 copy-done.1
  4.2 0.8 %copy.12.pv_ref = s32[384,64]{1,0:T(8,128)} copy(s32[384,64]{0,1:T(8,128)S(1)} %copy-done.1) | data formatting | bytes 196608 | tf_op args[7]
  5.0 58.2 %shard_map.95 = (bf16[768,64]{1,0:T(8,128)(2,1)}, f32[2,32,128]{2,1,0:T(8,128)}) custom-call(bf16[768,1024]{1,0:T(8,128)(2,1)} %x_ref.1, bf16[768,1024]{1,0:T(8,128)(2,1)} %g_ref.1, f32[1,1024]{1,0:T(1,128)} %bitcast.17, bf16[1024,256]{1,0:T(8,128)(2,1)} %pad_maximum_fusion.w_ref, s32[32]{0:T(128)} %counts_ref.1, s32[12,9]{1,0:T(8,128)} %nb_ref.1, ...), custom_call_target="tpu_custom_call" | custom-call | flops 4000000000 | bytes 5000000 | tf_op jit(solution)/shard_map/pallas_call | solution.py:455
  63.3 0.9 %slice_bitcast_fusion.7 = (f32[32,1,64]{2,0,1:T(8,128)S(1)}, f32[32,1,64]{2,0,1:T(8,128)S(1)}, f32[32,1,64]{2,0,1:T(8,128)S(1)}, f32[32,1,64]{2,0,1:T(8,128)S(1)}) fusion(f32[2,32,128]{2,1,0:T(8,128)} %get-tuple-element.5), kind=kLoop, calls=%fused_computation.10 | loop fusion | bytes 65536 | tf_op jit(solution)/shard_map/stack;squeeze | solution.py:524
  64.2 0.7 %copy.14 = f32[32,4,64]{2,1,0:T(4,128)} copy(f32[32,4,64]{2,0,1:T(8,128)S(1)} %pad_maximum_fusion.1) | data formatting | bytes 65536
  64.8 1.7 %copy.13 = bf16[768,64]{0,1:T(8,128)(2,1)} copy(bf16[768,64]{1,0:T(8,128)(2,1)} %get-tuple-element.6) | data formatting | bytes 196608
  (1 shorter events, 0.0 us)
Async XLA Ops:
  0.6 1.6 %copy-start = (bf16[1024,4,64]{0,2,1:T(8,128)(2,1)S(1)}, bf16[1024,4,64]{0,2,1:T(8,128)(2,1)}, u32[]{:S(2)}) copy-start(bf16[1024,4,64]{0,2,1:T(8,128)(2,1)} %param.12) | copy-start | bytes 1572868
  3.0 1.2 %copy-start.1 = (s32[384,64]{0,1:T(8,128)S(1)}, s32[384,64]{0,1:T(8,128)}, u32[]{:S(2)}) copy-start(s32[384,64]{0,1:T(8,128)} %param.15) | copy-start | bytes 294916

commit v2 on v1

v2 whole, which is shorter than its diff:
```python
import jax
import jax.numpy as jnp
from jax import lax
from jax.experimental import pallas as pl
from jax.experimental.pallas import tpu as pltpu
from jax.sharding import PartitionSpec as P

BF = jnp.bfloat16
F32 = jnp.float32
MESH = pl.DeviceIdType.MESH
OFF = -1e30

ROWS = 768
D = 1024
PIX = 64
CAP = 12
NB = 9
TILE = 256
HALF = 384
Z = 16
SLOTS = 384
Z_STEPS = (1, 15, 2, 14, 4, 8, 12)
NX = 4


def nn(a, b):
    return lax.dot_general(a, b, (((1,), (0,)), ((), ())), preferred_element_type=F32)


def nt(a, b):
    return lax.dot_general(a, b, (((1,), (1,)), ((), ())), preferred_element_type=F32)


def tile(i, size=TILE):
    if isinstance(i, int):
        return pl.ds(i * size, size)
    return pl.ds(pl.multiple_of(i * size, size), size)


def remote(src, dst, send_sem, recv_sem, **device):
    return pltpu.make_async_remote_copy(
        src_ref=src,
        dst_ref=dst,
        send_sem=send_sem,
        recv_sem=recv_sem,
        device_id=device,
        device_id_type=MESH,
    )


def kernel(
    x_hbm, g_hbm, gain_hbm, pw_hbm, wn_hbm, counts_ref, nb_hbm, pv_hbm,
    og_ref, pg_ref,
    x_ref, g_ref, gain_ref, pw_ref, wn_ref, nb_ref, pv_ref, wt, wk, hid, up, irms, fscale, nshare, ushare, kvw, kvt, kaug, qaug, qz, dz, q_t,
    sc, dp, mx, sums, pt, ds_t, halo_out, own_grad, halo_in, att_t, grads_t,
    m_out, m_in, pj, y_in, z_out, z_in, zb_out, zb_in,
    part, r1, s2, r2, r3, s3, r4,
    x_s, g_s, w_s, halo_s, halo_r, hg_s, hg_r, m_s, m_r, y_s, y_r, za_s, za_r, zb_s, zb_r,
    c_s, c_r, r2_s, r2_r, r3_s, r3_r, r4_s, r4_r,
):
    p = lax.axis_index("patch")
    t = lax.axis_index("tensor")
    y_lo, z = p // Z, p % Z
    core = t % 2
    x = (t // 2) % NX
    y_hi = t // 8
    right, left = (p + 1) % 32, (p + 31) % 32
    y_partner = (1 - y_lo) * Z + z
    row0 = t - x * 2
    x_right, x_left = row0 + ((x + 1) % NX) * 2, row0 + ((x + 3) % NX) * 2
    core_partner = t + 1 - 2 * core
    hi_partner = (t + 8) % 16

    def z_peer(r):
        return y_lo * Z + (z + r) % Z

    loads = [
        pltpu.make_async_copy(pw_hbm, pw_ref, w_s.at[0]),
        pltpu.make_async_copy(wn_hbm, wn_ref, w_s.at[1]),
        pltpu.make_async_copy(gain_hbm, gain_ref, w_s.at[2]),
    ]
    late_loads = [
        pltpu.make_async_copy(nb_hbm, nb_ref, w_s.at[3]),
        pltpu.make_async_copy(pv_hbm, pv_ref, w_s.at[4]),
        pltpu.make_async_copy(g_hbm, g_ref, g_s),
    ]

    def x_load(i):
        return pltpu.make_async_copy(x_hbm.at[tile(i), :], x_ref.at[tile(i), :], x_s.at[i])

    for load in loads:
        load.start()
    for i in range(3):
        x_load(i).start()
    for load in late_loads:
        load.start()

    barrier = pltpu.get_barrier_semaphore()

    def greet(r, carry):
        pl.semaphore_signal(barrier, inc=1, device_id={"tensor": (t + r) % 16}, device_id_type=MESH)
        return carry

    lax.fori_loop(1, 16, greet, 0)
    for other in (left, right, y_partner) + tuple(z_peer(r) for r in Z_STEPS):
        pl.semaphore_signal(barrier, inc=1, device_id={"patch": other}, device_id_type=MESH)

    for load in loads:
        load.wait()
    for to, at, size in ((0, 64, 128), (128, 0, 64), (192, 192, 64)):
        wt[to : to + size, :] = (
            pw_ref[at : at + size, :].astype(F32) + wn_ref[at : at + size, :].astype(F32)
        ).astype(BF)

    gain = gain_ref[...]

    def halo_copy(side, i):
        return remote(
            kvw.at[1, tile(i), :], kvw.at[2 * side, tile(i), :],
            halo_s.at[side, i], halo_r.at[side, i], patch=left if side else right,
        )

    def project(i):
        rows = tile(i)
        x_load(i).wait()
        xs = x_ref[rows, :].astype(F32)
        inv = lax.rsqrt(jnp.sum(xs * xs, axis=1, keepdims=True) * (1.0 / D) + 1e-06)
        h = (xs * inv * gain).astype(BF)
        hid[rows, :] = h
        irms[rows, :] = jnp.broadcast_to(inv, (TILE, 128))
        pr = nt(h, wt[...])
        kvw[1, rows, :] = pr[:, :128].astype(BF)
        if i == 0:
            pl.semaphore_wait(barrier, 25)
        halo_copy(0, i).start()
        halo_copy(1, i).start()
        lane = lax.broadcasted_iota(jnp.int32, (TILE, 128), 1)
        q = jnp.where(lane < 64, pr[:, 128:].astype(BF).astype(F32), 0.0)
        qz[rows, :] = (q * 0.125).astype(BF)
        q_t[:, rows] = jnp.transpose(q)[:64, :].astype(BF)

    for i in range(3):
        project(i)

    lane12 = lax.broadcasted_iota(jnp.int32, (CAP, 128), 1)
    for load in late_loads:
        load.wait()
    nb = nb_ref[...]
    member = lane12 == 64 + nb[:, 0:1]
    for j in range(1, NB):
        member = member | (lane12 == 64 + nb[:, j : j + 1])
    member = jnp.where(member, 0.0, OFF)
    member = jnp.where(lane12 == 100, 1.0, jnp.where(lane12 > 100, 0.0, member))
    lane64 = lax.broadcasted_iota(jnp.int32, (PIX, 128), 1)
    for b, owner in enumerate((left, p, right)):
        valid = pltpu.roll(pv_ref[...], SLOTS - owner * CAP, 1)[:, :128]
        valid = jnp.where(valid > 0, 0.0, OFF)
        for s in range(CAP):
            aux = jnp.where(lane64 == 64 + b * CAP + s, 1.0, 0.0)
            aux = jnp.where(lane64 == 100, valid[:, s : s + 1], aux)
            kaug[b, s * PIX : (s + 1) * PIX, :] = aux.astype(BF)

    live = counts_ref[p] * PIX

    def upstream(i, carry):
        rows = tile(i)
        row = lax.broadcasted_iota(jnp.int32, (TILE, 1), 0) + i * TILE
        g = jnp.where(row < live, g_ref[rows, :].astype(F32), 0.0).astype(BF)
        up[rows, :] = g
        og = nt(g, wt[128:256, :])
        lane = lax.broadcasted_iota(jnp.int32, (TILE, 128), 1)
        dz[rows, :] = jnp.where(lane >= 64, og, 0.0).astype(BF)
        return carry

    lax.fori_loop(0, 3, upstream, 0)
    for s in range(CAP):
        rows = slice(s * PIX, (s + 1) * PIX)
        qaug[rows, :] = jnp.where(lane64 < 64, qz[rows, :].astype(F32), member[s : s + 1, :]).astype(BF)

    def fold(value, op):
        return op(value.reshape(value.shape[0] // 8, 8, value.shape[1]), axis=0)

    def score(b):
        base = b * ROWS
        for i in range(3):
            rows = tile(i)
            kv = kvw[b, rows, :].astype(F32)
            lane = lax.broadcasted_iota(jnp.int32, (TILE, 128), 1)
            kaug[b, rows, :] = jnp.where(lane < 64, kv, kaug[b, rows, :].astype(F32)).astype(BF)
            kvt[b, :, rows] = jnp.transpose(kv).astype(BF)
        for q in range(3):
            cols = tile(q)
            s = nt(kaug[b], qaug[cols, :])
            sc[base : base + ROWS, cols] = s
            mx[b, :, cols] = fold(s, jnp.max)
            dp[base : base + ROWS, cols] = nt(kvw[b], dz[cols, :])

    def raise_block(b, q, top):
        cols = tile(q)
        total = jnp.zeros((8, TILE), F32)
        weighted = jnp.zeros((8, TILE), F32)
        for i in range(3):
            rows = tile(b * 3 + i)
            e = jnp.exp(sc[rows, cols] - top)
            sc[rows, cols] = e
            total = total + fold(e, jnp.sum)
            weighted = weighted + fold(e * dp[rows, cols], jnp.sum)
        return total, weighted

    def divide_block(b, q, inv, delta):
        cols = tile(q)
        for i in range(3):
            rows = tile(b * 3 + i)
            att = sc[rows, cols] * inv
            pt[rows, cols] = att.astype(BF)
            ds_t[rows, cols] = (att * (dp[rows, cols] - delta)).astype(BF)

    score(1)
    for q in range(3):
        cols = tile(q)
        top = jnp.max(mx[1, :, cols], axis=0, keepdims=True)
        sums[0, :, cols], sums[1, :, cols] = raise_block(1, q, top)

    odd = core == 1
    share = pl.ds(pl.multiple_of((t // 2) * 128, 128), 128)

    def mine(value):
        turned = jnp.transpose(value)
        return jnp.where(odd, turned[64:, :], turned[:64, :])

    gain_share = mine(jnp.broadcast_to(gain_ref[:, share], (128, 128)))[:, :1]

    def shares(i, carry):
        rows = tile(i)
        inv = jnp.transpose(irms[rows, :])[:1, :]
        fscale[:, rows] = gain_share * inv
        nshare[:, rows] = mine(x_ref[rows, share].astype(F32)) * (inv * inv)
        ushare[:, rows] = mine(up[rows, share].astype(F32))
        return carry

    lax.fori_loop(0, 3, shares, 0)

    order = [(2, 0), (2, 1), (1, 0), (3, 0), (0, 0), (1, 1), (3, 1), (0, 1)]

    def block_of(o):
        dx, k = order[o]
        y = (1 - y_hi) if k == 0 else y_hi
        return y * NX + (x + dx) % NX

    for o in range(8):
        wk[o * 128 : (o + 1) * 128, :] = jnp.transpose(wt[:, tile(block_of(o), 128)].astype(F32)).astype(BF)

    for side in range(2):
        for i in range(3):
            halo_copy(side, i).wait_recv()
        score(2 * side)

    def row(value):
        return jnp.max(value, axis=0, keepdims=True)

    own_scale = []
    for q in range(3):
        cols = tile(q)
        own_top = row(mx[1, :, cols])
        top = jnp.maximum(own_top, jnp.maximum(row(mx[0, :, cols]), row(mx[2, :, cols])))
        shrink = jnp.exp(own_top - top)
        total, weighted = sums[0, :, cols] * shrink, sums[1, :, cols] * shrink
        for b in (0, 2):
            part_total, part_weighted = raise_block(b, q, top)
            total, weighted = total + part_total, weighted + part_weighted
        inv = 1.0 / jnp.sum(total, axis=0, keepdims=True)
        delta = jnp.sum(weighted, axis=0, keepdims=True) * inv
        for b in (0, 2):
            divide_block(b, q, inv, delta)
        own_scale.append((inv * shrink, delta))

    def near_grad(start, size):
        at = pl.ds(start, size)
        return nn(ds_t[at, :], qz[...]) + nn(pt[at, :], dz[...])

    def grad_copy(side, i):
        rows = pl.ds(i * HALF, HALF)
        return remote(
            halo_out.at[side, rows, :], halo_in.at[1 - side, rows, :],
            hg_s.at[side, i], hg_r.at[1 - side, i], patch=right if side else left,
        )

    for i in range(2):
        for side in range(2):
            rows = pl.ds(i * HALF, HALF)
            halo_out[side, rows, :] = near_grad(2 * side * ROWS + i * HALF, HALF).astype(BF)
            grad_copy(side, i).start()

    for q in range(3):
        divide_block(1, q, *own_scale[q])
    own_grad[...] = near_grad(ROWS, ROWS)

    def query_side(q, carry):
        cols = tile(q)
        qg = jnp.zeros((64, TILE), F32)
        at = jnp.zeros((64, TILE), F32)
        for b in range(3):
            rows = slice(b * ROWS, (b + 1) * ROWS)
            qg = qg + nn(kvt[b, 0:64, :], ds_t[rows, cols])
            at = at + nn(kvt[b, 64:128, :], pt[rows, cols])
        grads_t[128:192, cols] = (qg * 0.125).astype(BF)
        att_t[:, cols] = at.astype(BF)
        return carry

    for q in range(3):
        query_side(q, 0)

    def weight_qo(n, carry):
        cols = tile(n)
        both = jnp.concatenate(
            [nn(grads_t[128:192, :], hid[:, cols]), nn(att_t[...], up[:, cols])], axis=0
        )
        pj[0, cols, :] = jnp.transpose(both).astype(BF)
        return carry

    for n in range(4):
        weight_qo(n, 0)

    def y_copy(h):
        return remote(
            pj.at[h, tile(1 - y_lo, 512), :], y_in.at[h], y_s.at[h], y_r.at[h], patch=y_partner
        )

    y_copy(0).start()

    for i in range(2):
        for side in range(2):
            grad_copy(side, i).wait_recv()

    def collect(i, carry):
        rows = tile(i)
        total = (
            own_grad[rows, :] + halo_in[0, rows, :].astype(F32) + halo_in[1, rows, :].astype(F32)
        )
        kvg = jnp.transpose(total).astype(BF)
        grads_t[0:128, rows] = kvg
        prod = jnp.sum(kvg.astype(F32) * kvt[1, :, rows].astype(F32), axis=0, keepdims=True)
        qg = grads_t[128:192, rows].astype(F32) * q_t[:, rows].astype(F32)
        prod = prod + jnp.sum(qg, axis=0, keepdims=True)
        for j in range(2):
            m_out[pl.ds(2 * i + j, 1), :] = prod[:, j * 128 : (j + 1) * 128]
        return carry

    m_out[...] = jnp.zeros_like(m_out)
    for i in range(3):
        collect(i, 0)

    def core_copy(o):
        return remote(
            part.at[o, tile(1 - core, 64), :], r1.at[o], c_s.at[o], c_r.at[o], tensor=core_partner
        )

    for group in range(2):
        some = nn(wk[group * 512 : (group + 1) * 512, 0:192], grads_t[...])
        for n in range(4):
            o = group * 4 + n
            part[o] = some[n * 128 : (n + 1) * 128, :].astype(BF)
            core_copy(o).start()

    def m_send(r, carry):
        remote(m_out, m_in.at[r - 1], m_s, m_r, tensor=(t + r) % 16).start()
        return carry

    lax.fori_loop(1, 16, m_send, 0)

    def pair_sum(o):
        core_copy(o).wait_recv()
        return part[o, tile(core, 64), :].astype(F32) + r1[o].astype(F32)

    def r2_copy(k, side):
        half = slice(side * 32, side * 32 + 32)
        return remote(
            s2.at[k, half, :], r2.at[side, k], r2_s.at[side, k], r2_r.at[side, k],
            tensor=x_right if side == 0 else x_left,
        )

    def r3_copy(k, side, half):
        o = 2 + 3 * k + side
        rows = slice(half * 32, half * 32 + 32)
        return remote(
            s2.at[o, rows, :], r3.at[side, k, rows, :], r3_s.at[side, k, half], r3_r.at[side, k, half],
            tensor=x_right if side == 0 else x_left,
        )

    def a_copy(h, n):
        step = (1, 15, 2, 14)[n]
        rows = (slice(0, 128), slice(0, 128), slice(0, 64), slice(64, 128))[n]
        return remote(
            z_out.at[h, (z + step) % 4, rows, :], z_in.at[h, n, rows, :],
            za_s.at[h, n], za_r.at[h, n], patch=z_peer(step),
        )

    def b_copy(h, r):
        return remote(
            zb_out.at[h, tile((z // 4 + r) % 4, 32), :], zb_in.at[h, r - 1],
            zb_s.at[h, r - 1], zb_r.at[h, r - 1], patch=z_peer(4 * r),
        )

    def a_stage(h):
        y_copy(h).wait_recv()
        for d in range(Z):
            rows = pl.ds(pl.multiple_of(y_lo * 512 + d * 32, 32), 32)
            both = pj[h, rows, :].astype(F32) + y_in[h, d * 32 : d * 32 + 32, :].astype(F32)
            z_out[h, d % 4, (d // 4) * 32 : (d // 4) * 32 + 32, :] = both.astype(BF)
        for n in range(4):
            a_copy(h, n).start()

    def b_stage(h):
        for n in range(4):
            a_copy(h, n).wait_recv()
        for i in range(2):
            rows = slice(i * 64, i * 64 + 64)
            total = z_out[h, z % 4, rows, :].astype(F32)
            for n in (0, 1, 2 + i):
                total = total + z_in[h, n, rows, :].astype(F32)
            zb_out[h, rows, :] = total.astype(BF)
        for r in range(1, 4):
            b_copy(h, r).start()

    def z_total(h):
        total = zb_out[h, tile(z // 4, 32), :].astype(F32)
        for r in range(1, 4):
            b_copy(h, r).wait_recv()
            total = total + zb_in[h, r - 1].astype(F32)
        for half in range(2):
            pg_ref[:, (1, 2)[half] if h else (0, 3)[half], :] = total[:, half * 64 : half * 64 + 64]

    for k in range(2):
        s2[k] = pair_sum(k).astype(BF)
        for side in range(2):
            r2_copy(k, side).start()
    for k in range(2):
        for side in range(2):
            o = 2 + 3 * k + side
            s2[o] = pair_sum(o).astype(BF)
            r3_copy(k, side, 1 - side).start()
    a_stage(0)

    for n in range(4):
        cols = tile(n)
        pj[1, cols, :] = jnp.transpose(nn(grads_t[0:128, :], hid[:, cols])).astype(BF)
    y_copy(1).start()

    for k in range(2):
        for side in range(2):
            o = 2 + 3 * k + side
            half = slice(side * 32, side * 32 + 32)
            r2_copy(k, side).wait_recv()
            s2[o, half, :] = (
                pair_sum_again(part, r1, core, o, half) + r2[side, k].astype(F32)
            ).astype(BF)
            r3_copy(k, side, side).start()
    b_stage(0)
    a_stage(1)

    def x_sum(k):
        o = 4 + 3 * k
        total = pair_sum(o)
        for side in range(2):
            for half in range(2):
                r3_copy(k, side, half).wait_recv()
            total = total + r3[side, k].astype(F32)
        return total

    r4_copy = remote(s3, r4, r4_s, r4_r, tensor=hi_partner)
    s3[...] = x_sum(0).astype(BF)
    r4_copy.start()
    b_stage(1)
    z_total(0)
    feature = x_sum(1)
    z_total(1)

    pltpu.make_async_copy(m_in, m_in, m_r).wait()
    m = m_out[...]
    for r in range(15):
        m = m + m_in[r]
    m = m * (1.0 / D)
    mean = jnp.concatenate([m[i : i + 1, :] for i in range(6)], axis=1)

    r4_copy.wait_recv()
    feature = feature + r4[...].astype(F32)
    og_ref[...] = (ushare[...] + feature * fscale[...] - nshare[...] * mean).astype(BF)

    for side in range(2):
        for i in range(3):
            halo_copy(side, i).wait_send()
        for i in range(2):
            grad_copy(side, i).wait_send()
    for o in range(8):
        core_copy(o).wait_send()
    for k in range(2):
        for side in range(2):
            r2_copy(k, side).wait_send()
            for half in range(2):
                r3_copy(k, side, half).wait_send()
    r4_copy.wait_send()
    for h in range(2):
        y_copy(h).wait_send()
        for n in range(4):
            a_copy(h, n).wait_send()
        for r in range(1, 4):
            b_copy(h, r).wait_send()
    pltpu.make_async_copy(m_in, m_in, m_s).wait()


def pair_sum_again(part, r1, core, o, half):
    rows = pl.ds(pl.multiple_of(core * 64 + half.start, 32), 32)
    return part[o, rows, :].astype(F32) + r1[o, half, :].astype(F32)


def per_device(
    inputs, cotangent, norm_gain, proj_weight, weight_noise, patch_counts, neighbours, pixel_valid
):
    def turned(weight):
        return jnp.transpose(weight, (1, 2, 0)).reshape(4 * weight.shape[2], D)

    vmem = pl.BlockSpec(memory_space=pltpu.VMEM)
    smem = pl.BlockSpec(memory_space=pltpu.SMEM)
    hbm = pl.BlockSpec(memory_space=pl.ANY)
    V = pltpu.VMEM
    dma = pltpu.SemaphoreType.DMA
    grad, proj = pl.pallas_call(
        kernel,
        out_shape=(
            jax.ShapeDtypeStruct((64, ROWS), BF),
            jax.ShapeDtypeStruct((32, 4, 64), F32),
        ),
        in_specs=[hbm, hbm, hbm, hbm, hbm, smem, hbm, hbm],
        out_specs=(vmem, vmem),
        scratch_shapes=[
            V((ROWS, D), BF),
            V((ROWS, D), BF),
            V((1, D), F32),
            V((256, D), BF),
            V((256, D), BF),
            V((CAP, NB), jnp.int32),
            V((PIX, SLOTS), jnp.int32),
            V((256, D), BF),
            V((D, 256), BF),
            V((ROWS, D), BF),
            V((ROWS, D), BF),
            V((ROWS, 128), F32),
            V((64, ROWS), F32),
            V((64, ROWS), F32),
            V((64, ROWS), F32),
            V((3, ROWS, 128), BF),
            V((3, 128, ROWS), BF),
            V((3, ROWS, 128), BF),
            V((ROWS, 128), BF),
            V((ROWS, 128), BF),
            V((ROWS, 128), BF),
            V((64, ROWS), BF),
            V((3 * ROWS, ROWS), F32),
            V((3 * ROWS, ROWS), F32),
            V((3, 8, ROWS), F32),
            V((2, 8, ROWS), F32),
            V((3 * ROWS, ROWS), BF),
            V((3 * ROWS, ROWS), BF),
            V((2, ROWS, 128), BF),
            V((ROWS, 128), F32),
            V((2, ROWS, 128), BF),
            V((64, ROWS), BF),
            V((192, ROWS), BF),
            V((8, 128), F32),
            V((15, 8, 128), F32),
            V((2, D, 128), BF),
            V((2, 512, 128), BF),
            V((2, 4, 128, 128), BF),
            V((2, 4, 128, 128), BF),
            V((2, 128, 128), BF),
            V((2, 3, 32, 128), BF),
            V((8, 128, ROWS), BF),
            V((8, 64, ROWS), BF),
            V((8, 64, ROWS), BF),
            V((2, 2, 32, ROWS), BF),
            V((2, 2, 64, ROWS), BF),
            V((64, ROWS), BF),
            V((64, ROWS), BF),
            dma((3,)), dma, dma((5,)),
            dma((2, 3)), dma((2, 3)),
            dma((2, 2)), dma((2, 2)),
            dma, dma,
            dma((2,)), dma((2,)),
            dma((2, 4)), dma((2, 4)),
            dma((2, 3)), dma((2, 3)),
            dma((8,)), dma((8,)),
            dma((2, 2)), dma((2, 2)),
            dma((2, 2, 2)), dma((2, 2, 2)),
            dma, dma,
        ],
        compiler_params=pltpu.CompilerParams(
            collective_id=0, has_side_effects=True, vmem_limit_bytes=56 * 1024 * 1024
        ),
        cost_estimate=pl.CostEstimate(
            flops=4 * 10**9, bytes_accessed=5 * 10**6, transcendentals=2 * 10**6
        ),
    )(
        inputs,
        cotangent,
        norm_gain.reshape(1, D),
        turned(proj_weight),
        turned(weight_noise),
        patch_counts,
        neighbours,
        jnp.transpose(pixel_valid),
    )
    return (jnp.transpose(grad), proj)


def solution(mesh):
    placed = (
        P("patch", None),
        P("patch", None),
        P(),
        P(None, None, "tensor"),
        P(None, None, "tensor"),
        P(),
        P("patch", None),
        P(),
    )
    return jax.shard_map(
        per_device,
        mesh=mesh,
        in_specs=placed,
        out_specs=(P("patch", "tensor"), P("patch", None, "tensor")),
        check_vma=False,
    )
```

time: 66.8 us -> 56 us (0.84)
  Pallas kernels: 58.2 us -> 51.6 us
  local copies, waits for them, and re-layouts: 6.17 us -> 3.01 us
  other arithmetic: 1.43 us -> 0 us
    pallas_call x1, Pallas kernels: 58.2 us -> 51.6 us  [per_device(): pl.pallas_call(kernel, out_shape=(jax.ShapeDtypeStruct((64, ROWS), BF), j...]
    unnamed x9 -> x2, local copies, waits for them, and re-layouts: 5.23 us -> 3.01 us
    concatenate x1 -> x0, other arithmetic: 1.15 us -> none  [per_device(): jnp.concatenate([weights[:, 1], weights[:, 2], weights[:, 0], weights[:,...]
    another operation x1 -> x0, local copies, waits for them, and re-layouts: 0.88 us -> none  [per_device(): jnp.stack([proj[0, :, :64], proj[1, :, :64], proj[1, :, 64:], proj[0, :,...]
where the time goes in v2:
time: 56 us; the launch traced here: 55.2 us
  Pallas kernels  51.6 us (92%)
  local copies, waits for them, and re-layouts  3.01 us (5%)
  between operations  0.64 us (1%)
    pallas_call x1, Pallas kernels, per_device(): pl.pallas_call(kernel, out_shape=(jax.ShapeDtypeStruct((64, ROWS), BF), j...  51.6 us
    unnamed x2, local copies, waits for them, and re-layouts  3.01 us

profile of v2, /device:TPU:1, one launch (start us, length us, event | category | flops | bytes accessed | tf_op | source)
XLA Modules:
  0.0 55.2 jit_solution(3388923325499010644)
XLA Ops:
  0.6 51.6 %shard_map.95 = (bf16[64,768]{1,0:T(8,128)(2,1)}, f32[32,4,64]{2,1,0:T(4,128)}) custom-call(bf16[768,1024]{1,0:T(8,128)(2,1)} %x_hbm.1, bf16[768,1024]{1,0:T(8,128)(2,1)} %g_hbm.1, f32[1,1024]{1,0:T(1,128)} %bitcast.13, bf16[256,1024]{1,0:T(8,128)(2,1)} %bitcast.10, bf16[256,1024]{1,0:T(8,128)(2,1)} %bitcast.11, s32[32]{0:T(128)} %counts_ref.1, ...), custom_call_target="tpu_custom_call" | custom-call | flops 4000000000 | bytes 5000000 | tf_op jit(solution)/shard_map/pallas_call | solution.py:527
  52.2 1.5 %copy.12 = bf16[768,64]{0,1:T(8,128)(2,1)} copy(bf16[768,64]{0,1:T(8,128)(2,1)} %bitcast.9) | data formatting | bytes 196608
  53.7 1.5 %copy.13 = f32[32,4,64]{2,1,0:T(4,128)} copy(f32[32,4,64]{2,1,0:T(4,128)} %get-tuple-element.9) | data formatting | bytes 65536

commit v3 on v2

v3 whole, which is shorter than its diff:
```python
import jax
import jax.numpy as jnp
from jax import lax
from jax.experimental import pallas as pl
from jax.experimental.pallas import tpu as pltpu
from jax.sharding import PartitionSpec as P

BF = jnp.bfloat16
F32 = jnp.float32
MESH = pl.DeviceIdType.MESH
OFF = -1e30

ROWS = 768
D = 1024
PIX = 64
CAP = 12
NB = 9
TILE = 256
Z = 16
SLOTS = 384
NX = 4


def nn(a, b):
    return lax.dot_general(a, b, (((1,), (0,)), ((), ())), preferred_element_type=F32)


def nt(a, b):
    return lax.dot_general(a, b, (((1,), (1,)), ((), ())), preferred_element_type=F32)


def tile(i, size=TILE):
    if isinstance(i, int):
        return pl.ds(i * size, size)
    return pl.ds(pl.multiple_of(i * size, size), size)


def remote(src, dst, send_sem, recv_sem, **device):
    return pltpu.make_async_remote_copy(
        src_ref=src,
        dst_ref=dst,
        send_sem=send_sem,
        recv_sem=recv_sem,
        device_id=device,
        device_id_type=MESH,
    )


def kernel(
    x_hbm, g_hbm, gain_hbm, pw_hbm, wn_hbm, counts_hbm, nb_hbm, pv_hbm,
    og_ref, pg_ref,
    x_ref, g_ref, gain_ref, pw_ref, wn_ref, counts_ref, nb_ref, pv_ref, wt, wk, hid, up, irms, fscale, nshare, ushare, kvw, kvt, kaug, qaug, qz, dz, q_t,
    sc, dp, mx, sums, pt, ds_t, halo_out, own_grad, halo_in, att_t, grads_t,
    m_out, m_in, pj, a_in, b_out, b_in,
    part, r1, s2, r2,
    x_s, g_s, w_s, halo_s, halo_r, hg_s, hg_r, m_s, m_r, a_s, a_r, b_s, b_r,
    c_s, c_r, r2_s, r2_r, known,
):
    p = lax.axis_index("patch")
    t = lax.axis_index("tensor")
    y_lo, z = p // Z, p % Z
    core = t % 2
    x = (t // 2) % NX
    y_hi = t // 8
    right, left = (p + 1) % 32, (p + 31) % 32
    core_partner = t + 1 - 2 * core

    def z_peer(r, other=0):
        return (1 - y_lo if other else y_lo) * Z + (z + r) % Z

    loads = [
        pltpu.make_async_copy(pw_hbm, pw_ref, w_s.at[0]),
        pltpu.make_async_copy(wn_hbm, wn_ref, w_s.at[1]),
        pltpu.make_async_copy(gain_hbm, gain_ref, w_s.at[2]),
    ]
    late_loads = [
        pltpu.make_async_copy(counts_hbm, counts_ref, w_s.at[5]),
        pltpu.make_async_copy(nb_hbm, nb_ref, w_s.at[3]),
        pltpu.make_async_copy(pv_hbm, pv_ref, w_s.at[4]),
        pltpu.make_async_copy(g_hbm, g_ref, g_s),
    ]

    def x_load(i):
        return pltpu.make_async_copy(x_hbm.at[tile(i), :], x_ref.at[tile(i), :], x_s.at[i])

    for load in loads:
        load.start()
    for i in range(3):
        x_load(i).start()
    for load in late_loads:
        load.start()

    barrier = pltpu.get_barrier_semaphore()

    def patch_of(r, other=0):
        return {"patch": z_peer(r, other)}

    row0 = t - x * 2
    near = [
        {"patch": left}, {"patch": right}, {"tensor": core_partner},
        {"tensor": row0 + (x + 1) % NX * 2}, {"tensor": row0 + (x + 3) % NX * 2},
        {"tensor": (t + 8) % 16}, patch_of(0, 1), patch_of(1), patch_of(15),
    ]
    rounds = [near, near + [patch_of(2), patch_of(14)], [near[2], patch_of(4), patch_of(12)]]

    def tell(semaphore, partners):
        for device in partners:
            pl.semaphore_signal(semaphore, inc=1, device_id=device, device_id_type=MESH)

    def tell_round(n):
        tell(known.at[n], rounds[n])

    def hear_round(n):
        pl.semaphore_wait(known.at[n], len(rounds[n]))

    tell(barrier, near)

    for load in loads:
        load.wait()
    for to, at, size in ((0, 64, 128), (128, 0, 64), (192, 192, 64)):
        wt[to : to + size, :] = (
            pw_ref[at : at + size, :].astype(F32) + wn_ref[at : at + size, :].astype(F32)
        ).astype(BF)

    gain = gain_ref[...]

    def halo_copy(side, i):
        return remote(
            kvw.at[1, tile(i), :], kvw.at[2 * side, tile(i), :],
            halo_s.at[side, i], halo_r.at[side, i], patch=left if side else right,
        )

    def project(i):
        rows = tile(i)
        x_load(i).wait()
        xs = x_ref[rows, :].astype(F32)
        inv = lax.rsqrt(jnp.sum(xs * xs, axis=1, keepdims=True) * (1.0 / D) + 1e-06)
        h = (xs * inv * gain).astype(BF)
        hid[rows, :] = h
        irms[rows, :] = jnp.broadcast_to(inv, (TILE, 128))
        pr = nt(h, wt[...])
        kvw[1, rows, :] = pr[:, :128].astype(BF)
        if i == 0:
            pl.semaphore_wait(barrier, len(near))
            tell_round(0)
        halo_copy(0, i).start()
        halo_copy(1, i).start()
        lane = lax.broadcasted_iota(jnp.int32, (TILE, 128), 1)
        q = jnp.where(lane < 64, pr[:, 128:].astype(BF).astype(F32), 0.0)
        qz[rows, :] = (q * 0.125).astype(BF)
        q_t[:, rows] = jnp.transpose(q)[:64, :].astype(BF)

    for i in range(3):
        project(i)

    lane12 = lax.broadcasted_iota(jnp.int32, (CAP, 128), 1)
    for load in late_loads:
        load.wait()
    nb = nb_ref[...]
    member = lane12 == 64 + nb[:, 0:1]
    for j in range(1, NB):
        member = member | (lane12 == 64 + nb[:, j : j + 1])
    member = jnp.where(member, 0.0, OFF)
    member = jnp.where(lane12 == 100, 1.0, jnp.where(lane12 > 100, 0.0, member))
    lane64 = lax.broadcasted_iota(jnp.int32, (PIX, 128), 1)
    for b, owner in enumerate((left, p, right)):
        valid = pltpu.roll(pv_ref[...], SLOTS - owner * CAP, 1)[:, :128]
        valid = jnp.where(valid > 0, 0.0, OFF)
        for s in range(CAP):
            aux = jnp.where(lane64 == 64 + b * CAP + s, 1.0, 0.0)
            aux = jnp.where(lane64 == 100, valid[:, s : s + 1], aux)
            kaug[b, s * PIX : (s + 1) * PIX, :] = aux.astype(BF)

    live = counts_ref[p] * PIX

    def upstream(i, carry):
        rows = tile(i)
        row = lax.broadcasted_iota(jnp.int32, (TILE, 1), 0) + i * TILE
        g = jnp.where(row < live, g_ref[rows, :].astype(F32), 0.0).astype(BF)
        up[rows, :] = g
        og = nt(g, wt[128:256, :])
        lane = lax.broadcasted_iota(jnp.int32, (TILE, 128), 1)
        dz[rows, :] = jnp.where(lane >= 64, og, 0.0).astype(BF)
        return carry

    lax.fori_loop(0, 3, upstream, 0)
    for s in range(CAP):
        rows = slice(s * PIX, (s + 1) * PIX)
        qaug[rows, :] = jnp.where(lane64 < 64, qz[rows, :].astype(F32), member[s : s + 1, :]).astype(BF)

    def fold(value, op):
        return op(value.reshape(value.shape[0] // 8, 8, value.shape[1]), axis=0)

    def score(b, i):
        rows = tile(i)
        at = tile(b * 3 + i)
        kv = kvw[b, rows, :].astype(F32)
        lane = lax.broadcasted_iota(jnp.int32, (TILE, 128), 1)
        kaug[b, rows, :] = jnp.where(lane < 64, kv, kaug[b, rows, :].astype(F32)).astype(BF)
        kvt[b, :, rows] = jnp.transpose(kv).astype(BF)
        for q in range(3):
            cols = tile(q)
            s = nt(kaug[b, rows, :], qaug[cols, :])
            sc[at, cols] = s
            mx[b * 3 + i, :, cols] = fold(s, jnp.max)
            dp[at, cols] = nt(kvw[b, rows, :], dz[cols, :])

    def top_of(b, cols):
        return jnp.max(jnp.max(mx[b * 3 : b * 3 + 3, :, cols], axis=0), axis=0, keepdims=True)

    def raise_block(b, q, top):
        cols = tile(q)
        total = jnp.zeros((8, TILE), F32)
        weighted = jnp.zeros((8, TILE), F32)
        for i in range(3):
            rows = tile(b * 3 + i)
            e = jnp.exp(sc[rows, cols] - top)
            sc[rows, cols] = e
            total = total + fold(e, jnp.sum)
            weighted = weighted + fold(e * dp[rows, cols], jnp.sum)
        return total, weighted

    def divide_block(b, q, inv, delta):
        cols = tile(q)
        for i in range(3):
            rows = tile(b * 3 + i)
            att = sc[rows, cols] * inv
            pt[rows, cols] = att.astype(BF)
            ds_t[rows, cols] = (att * (dp[rows, cols] - delta)).astype(BF)

    hear_round(0)
    tell_round(1)

    for i in range(3):
        score(1, i)
    for q in range(3):
        cols = tile(q)
        sums[0, :, cols], sums[1, :, cols] = raise_block(1, q, top_of(1, cols))

    for i in range(3):
        for side in range(2):
            halo_copy(side, i).wait_recv()
            score(2 * side, i)

    scales = []
    for q in range(3):
        cols = tile(q)
        own_top = top_of(1, cols)
        top = jnp.maximum(own_top, jnp.maximum(top_of(0, cols), top_of(2, cols)))
        shrink = jnp.exp(own_top - top)
        total, weighted = sums[0, :, cols] * shrink, sums[1, :, cols] * shrink
        for b in (0, 2):
            part_total, part_weighted = raise_block(b, q, top)
            total, weighted = total + part_total, weighted + part_weighted
        inv = 1.0 / jnp.sum(total, axis=0, keepdims=True)
        delta = jnp.sum(weighted, axis=0, keepdims=True) * inv
        scales.append((inv, inv * shrink, delta))

    def near_grad(b):
        at = tile(b, ROWS)
        return nn(ds_t[at, :], qz[...]) + nn(pt[at, :], dz[...])

    def grad_copy(side):
        return remote(
            halo_out.at[side], halo_in.at[1 - side], hg_s.at[side], hg_r.at[1 - side],
            patch=right if side else left,
        )

    for side in range(2):
        for q in range(3):
            divide_block(2 * side, q, scales[q][0], scales[q][2])
        halo_out[side] = near_grad(2 * side).astype(BF)
        grad_copy(side).start()

    for q in range(3):
        divide_block(1, q, scales[q][1], scales[q][2])
    own_grad[...] = near_grad(1)

    def query_side(q, carry):
        cols = tile(q)
        qg = jnp.zeros((64, TILE), F32)
        at = jnp.zeros((64, TILE), F32)
        for b in range(3):
            rows = slice(b * ROWS, (b + 1) * ROWS)
            qg = qg + nn(kvt[b, 0:64, :], ds_t[rows, cols])
            at = at + nn(kvt[b, 64:128, :], pt[rows, cols])
        grads_t[128:192, cols] = (qg * 0.125).astype(BF)
        att_t[:, cols] = at.astype(BF)
        return carry

    for q in range(3):
        query_side(q, 0)

    def put(h, n, value):
        for j in range(8):
            y, d = divmod(n * 8 + j, Z)
            pj[h, y, d % 4, (d // 4) * 32 : (d // 4) * 32 + 32, :] = value[j * 32 : j * 32 + 32, :]

    whole, first, last = slice(0, 128), slice(0, 64), slice(64, 128)
    window = [
        (1, 2, first), (1, 14, last), (0, 2, first), (0, 14, last),
        (1, 1, whole), (1, 15, whole), (1, 0, whole), (0, 1, whole), (0, 15, whole),
    ]

    def a_copy(h, n):
        other, step, rows = window[n]
        return remote(
            pj.at[h, 1 - y_lo if other else y_lo, (z + step) % 4, rows, :], a_in.at[h, n, rows, :],
            a_s.at[h, n], a_r.at[h, n], patch=z_peer(step, other),
        )

    def b_copy(h, r):
        return remote(
            b_out.at[h, tile((z // 4 + r) % 4, 32), :], b_in.at[h, r - 1],
            b_s.at[h, r - 1], b_r.at[h, r - 1], patch=z_peer(4 * r),
        )

    def a_stage(h):
        for n in range(9):
            a_copy(h, n).start()

    def b_stage(h):
        for n in range(9):
            a_copy(h, n).wait_recv()
        for i, rows in enumerate((first, last)):
            total = pj[h, y_lo, z % 4, rows, :].astype(F32)
            for n in (i, 2 + i, 4, 5, 6, 7, 8):
                total = total + a_in[h, n, rows, :].astype(F32)
            b_out[h, rows, :] = total.astype(BF)
        for r in (2, 1, 3):
            b_copy(h, r).start()

    def z_total(h):
        total = b_out[h, tile(z // 4, 32), :].astype(F32)
        for r in range(1, 4):
            b_copy(h, r).wait_recv()
            total = total + b_in[h, r - 1].astype(F32)
        for half in range(2):
            pg_ref[:, (1, 2)[half] if h else (0, 3)[half], :] = total[:, half * 64 : half * 64 + 64]

    for n in range(4):
        cols = tile(n)
        both = jnp.concatenate(
            [nn(grads_t[128:192, :], hid[:, cols]), nn(att_t[...], up[:, cols])], axis=0
        )
        put(0, n, jnp.transpose(both).astype(BF))
    hear_round(1)
    tell_round(2)
    a_stage(0)

    odd = core == 1
    share = pl.ds(pl.multiple_of((t // 2) * 128, 128), 128)

    def mine(value):
        turned = jnp.transpose(value)
        return jnp.where(odd, turned[64:, :], turned[:64, :])

    gain_share = mine(jnp.broadcast_to(gain_ref[:, share], (128, 128)))[:, :1]

    def shares(i, carry):
        rows = tile(i)
        inv = jnp.transpose(irms[rows, :])[:1, :]
        fscale[:, rows] = gain_share * inv
        nshare[:, rows] = mine(x_ref[rows, share].astype(F32)) * (inv * inv)
        ushare[:, rows] = mine(up[rows, share].astype(F32))
        return carry

    lax.fori_loop(0, 3, shares, 0)

    order = [(2, 0), (2, 1), (1, 0), (3, 0), (0, 0), (1, 1), (3, 1), (0, 1)]

    def block_of(o):
        dx, k = order[o]
        y = (1 - y_hi) if k == 0 else y_hi
        return y * NX + (x + dx) % NX

    for o in range(8):
        wk[o * 128 : (o + 1) * 128, :] = jnp.transpose(wt[:, tile(block_of(o), 128)].astype(F32)).astype(BF)

    for side in range(2):
        grad_copy(side).wait_recv()

    def collect(i, carry):
        rows = tile(i)
        total = (
            own_grad[rows, :] + halo_in[0, rows, :].astype(F32) + halo_in[1, rows, :].astype(F32)
        )
        kvg = jnp.transpose(total).astype(BF)
        grads_t[0:128, rows] = kvg
        prod = jnp.sum(kvg.astype(F32) * kvt[1, :, rows].astype(F32), axis=0, keepdims=True)
        qg = grads_t[128:192, rows].astype(F32) * q_t[:, rows].astype(F32)
        prod = prod + jnp.sum(qg, axis=0, keepdims=True)
        for j in range(2):
            m_out[pl.ds(2 * i + j, 1), :] = prod[:, j * 128 : (j + 1) * 128]
        return carry

    m_out[...] = jnp.zeros_like(m_out)
    for i in range(3):
        collect(i, 0)

    def core_copy(o):
        return remote(
            part.at[o, tile(1 - core, 64), :], r1.at[o], c_s.at[o], c_r.at[o], tensor=core_partner
        )

    def part_group(group):
        some = nn(wk[group * 512 : (group + 1) * 512, 0:192], grads_t[...])
        for n in range(4):
            o = group * 4 + n
            part[o] = some[n * 128 : (n + 1) * 128, :].astype(BF)
            core_copy(o).start()

    for n in range(4):
        put(1, n, jnp.transpose(nn(grads_t[0:128, :], hid[:, tile(n)])).astype(BF))
    a_stage(1)
    part_group(0)
    part_group(1)
    hear_round(2)

    def m_send(r, carry):
        remote(m_out, m_in.at[r - 1], m_s, m_r, tensor=(t + r) % 16).start()
        return carry

    lax.fori_loop(1, 16, m_send, 0)

    def pair_sum(o):
        core_copy(o).wait_recv()
        return part[o, tile(core, 64), :].astype(F32) + r1[o].astype(F32)

    def chip_copy(o):
        return remote(
            s2.at[o], r2.at[o], r2_s.at[o], r2_r.at[o], tensor=block_of(o) * 2 + core
        )

    for o in range(7):
        s2[o] = pair_sum(o).astype(BF)
        chip_copy(o).start()
    b_stage(0)
    feature = pair_sum(7)
    b_stage(1)
    z_total(0)

    pltpu.make_async_copy(m_in, m_in, m_r).wait()
    m = m_out[...]
    for r in range(15):
        m = m + m_in[r]
    m = m * (1.0 / D)
    mean = jnp.concatenate([m[i : i + 1, :] for i in range(6)], axis=1)

    for o in range(7):
        chip_copy(o).wait_recv()
        feature = feature + r2[o].astype(F32)
    og_ref[...] = (ushare[...] + feature * fscale[...] - nshare[...] * mean).astype(BF)
    z_total(1)

    for side in range(2):
        for i in range(3):
            halo_copy(side, i).wait_send()
        grad_copy(side).wait_send()
    for o in range(8):
        core_copy(o).wait_send()
    for o in range(7):
        chip_copy(o).wait_send()
    for h in range(2):
        for n in range(9):
            a_copy(h, n).wait_send()
        for r in range(1, 4):
            b_copy(h, r).wait_send()
    pltpu.make_async_copy(m_in, m_in, m_s).wait()


def per_device(
    inputs, cotangent, norm_gain, proj_weight, weight_noise, patch_counts, neighbours, pixel_valid
):
    def turned(weight):
        return jnp.transpose(weight, (1, 2, 0)).reshape(4 * weight.shape[2], D)

    vmem = pl.BlockSpec(memory_space=pltpu.VMEM)
    hbm = pl.BlockSpec(memory_space=pl.ANY)
    V = pltpu.VMEM
    dma = pltpu.SemaphoreType.DMA
    grad, proj = pl.pallas_call(
        kernel,
        out_shape=(
            jax.ShapeDtypeStruct((64, ROWS), BF),
            jax.ShapeDtypeStruct((32, 4, 64), F32),
        ),
        in_specs=[hbm] * 8,
        out_specs=(vmem, vmem),
        scratch_shapes=[
            V((ROWS, D), BF),
            V((ROWS, D), BF),
            V((1, D), F32),
            V((256, D), BF),
            V((256, D), BF),
            pltpu.SMEM((32,), jnp.int32),
            V((CAP, NB), jnp.int32),
            V((PIX, SLOTS), jnp.int32),
            V((256, D), BF),
            V((D, 256), BF),
            V((ROWS, D), BF),
            V((ROWS, D), BF),
            V((ROWS, 128), F32),
            V((64, ROWS), F32),
            V((64, ROWS), F32),
            V((64, ROWS), F32),
            V((3, ROWS, 128), BF),
            V((3, 128, ROWS), BF),
            V((3, ROWS, 128), BF),
            V((ROWS, 128), BF),
            V((ROWS, 128), BF),
            V((ROWS, 128), BF),
            V((64, ROWS), BF),
            V((3 * ROWS, ROWS), F32),
            V((3 * ROWS, ROWS), F32),
            V((9, 8, ROWS), F32),
            V((2, 8, ROWS), F32),
            V((3 * ROWS, ROWS), BF),
            V((3 * ROWS, ROWS), BF),
            V((2, ROWS, 128), BF),
            V((ROWS, 128), F32),
            V((2, ROWS, 128), BF),
            V((64, ROWS), BF),
            V((192, ROWS), BF),
            V((8, 128), F32),
            V((15, 8, 128), F32),
            V((2, 2, 4, 128, 128), BF),
            V((2, 9, 128, 128), BF),
            V((2, 128, 128), BF),
            V((2, 3, 32, 128), BF),
            V((8, 128, ROWS), BF),
            V((8, 64, ROWS), BF),
            V((7, 64, ROWS), BF),
            V((7, 64, ROWS), BF),
            dma((3,)), dma, dma((6,)),
            dma((2, 3)), dma((2, 3)),
            dma((2,)), dma((2,)),
            dma, dma,
            dma((2, 9)), dma((2, 9)),
            dma((2, 3)), dma((2, 3)),
            dma((8,)), dma((8,)),
            dma((7,)), dma((7,)),
            pltpu.SemaphoreType.REGULAR((3,)),
        ],
        compiler_params=pltpu.CompilerParams(
            collective_id=0, has_side_effects=True, vmem_limit_bytes=56 * 1024 * 1024
        ),
        cost_estimate=pl.CostEstimate(
            flops=4 * 10**9, bytes_accessed=5 * 10**6, transcendentals=2 * 10**6
        ),
    )(
        inputs,
        cotangent,
        norm_gain.reshape(1, D),
        turned(proj_weight),
        turned(weight_noise),
        patch_counts,
        neighbours,
        jnp.transpose(pixel_valid),
    )
    return (jnp.transpose(grad), proj)


def solution(mesh):
    placed = (
        P("patch", None),
        P("patch", None),
        P(),
        P(None, None, "tensor"),
        P(None, None, "tensor"),
        P(),
        P("patch", None),
        P(),
    )
    return jax.shard_map(
        per_device,
        mesh=mesh,
        in_specs=placed,
        out_specs=(P("patch", "tensor"), P("patch", None, "tensor")),
        check_vma=False,
    )
```

time: 56 us -> 51.9 us (0.927)
  Pallas kernels: 51.6 us -> 48 us
    pallas_call x1, Pallas kernels: 51.6 us -> 48 us  [per_device(): pl.pallas_call(kernel, out_shape=(jax.ShapeDtypeStruct((64, ROWS), BF), j...]
where the time goes in v3:
time: 51.9 us; the launch traced here: 51.7 us
  Pallas kernels  48 us (92%)
  local copies, waits for them, and re-layouts  3.01 us (6%)
  between operations  0.64 us (1%)
    pallas_call x1, Pallas kernels, per_device(): pl.pallas_call(kernel, out_shape=(jax.ShapeDtypeStruct((64, ROWS), BF), j...  48 us
    unnamed x2, local copies, waits for them, and re-layouts  3.01 us

profile of v3, /device:TPU:1, one launch (start us, length us, event | category | flops | bytes accessed | tf_op | source)
XLA Modules:
  0.0 51.7 jit_solution(5104019701923744575)
XLA Ops:
  0.6 48.0 %shard_map.95 = (bf16[64,768]{1,0:T(8,128)(2,1)}, f32[32,4,64]{2,1,0:T(4,128)}) custom-call(bf16[768,1024]{1,0:T(8,128)(2,1)} %x_hbm.1, bf16[768,1024]{1,0:T(8,128)(2,1)} %g_hbm.1, f32[1,1024]{1,0:T(1,128)} %bitcast.13, bf16[256,1024]{1,0:T(8,128)(2,1)} %bitcast.10, bf16[256,1024]{1,0:T(8,128)(2,1)} %bitcast.11, s32[32]{0:T(128)} %counts_hbm.1, ...), custom_call_target="tpu_custom_call" | custom-call | flops 4000000000 | bytes 5000000 | tf_op jit(solution)/shard_map/pallas_call | solution.py:482
  48.6 1.5 %copy.12 = bf16[768,64]{0,1:T(8,128)(2,1)} copy(bf16[768,64]{0,1:T(8,128)(2,1)} %bitcast.9) | data formatting | bytes 196608
  50.2 1.5 %copy.13 = f32[32,4,64]{2,1,0:T(4,128)} copy(f32[32,4,64]{2,1,0:T(4,128)} %get-tuple-element.9) | data formatting | bytes 65536

commit v4 on v3

--- a/solution.py
+++ b/solution.py
@@ -49,7 +49,7 @@
 def kernel(
     x_hbm, g_hbm, gain_hbm, pw_hbm, wn_hbm, counts_hbm, nb_hbm, pv_hbm,
     og_ref, pg_ref,
-    x_ref, g_ref, gain_ref, pw_ref, wn_ref, counts_ref, nb_ref, pv_ref, wt, wk, hid, up, irms, fscale, nshare, ushare, kvw, kvt, kaug, qaug, qz, dz, q_t,
+    x_ref, g_ref, gain_ref, pw_ref, wn_ref, counts_ref, nb_ref, pv_ref, wt, wk, hid, up, irms, fscale, nshare, ushare, kvw, kvt, kaug, qaug, q_raw, qz, dz, q_t,
     sc, dp, mx, sums, pt, ds_t, halo_out, own_grad, halo_in, att_t, grads_t,
     m_out, m_in, pj, a_in, b_out, b_in,
     part, r1, s2, r2,
@@ -69,9 +69,9 @@
         return (1 - y_lo if other else y_lo) * Z + (z + r) % Z
 
     loads = [
+        pltpu.make_async_copy(gain_hbm, gain_ref, w_s.at[2]),
         pltpu.make_async_copy(pw_hbm, pw_ref, w_s.at[0]),
         pltpu.make_async_copy(wn_hbm, wn_ref, w_s.at[1]),
-        pltpu.make_async_copy(gain_hbm, gain_ref, w_s.at[2]),
     ]
     late_loads = [
         pltpu.make_async_copy(counts_hbm, counts_ref, w_s.at[5]),
@@ -83,9 +83,10 @@
     def x_load(i):
         return pltpu.make_async_copy(x_hbm.at[tile(i), :], x_ref.at[tile(i), :], x_s.at[i])
 
+    x_load(0).start()
     for load in loads:
         load.start()
-    for i in range(3):
+    for i in range(1, 3):
         x_load(i).start()
     for load in late_loads:
         load.start()
@@ -115,43 +116,52 @@
 
     tell(barrier, near)
 
-    for load in loads:
+    def norm(i):
+        rows = tile(i)
+        x_load(i).wait()
+        xs = x_ref[rows, :].astype(F32)
+        inv = lax.rsqrt(jnp.sum(xs * xs, axis=1, keepdims=True) * (1.0 / D) + 1e-06)
+        hid[rows, :] = (xs * inv * gain_ref[...]).astype(BF)
+        irms[rows, :] = jnp.broadcast_to(inv, (TILE, 128))
+
+    loads[0].wait()
+    norm(0)
+
+    for load in loads[1:]:
         load.wait()
     for to, at, size in ((0, 64, 128), (128, 0, 64), (192, 192, 64)):
         wt[to : to + size, :] = (
             pw_ref[at : at + size, :].astype(F32) + wn_ref[at : at + size, :].astype(F32)
         ).astype(BF)
 
-    gain = gain_ref[...]
-
     def halo_copy(side, i):
         return remote(
             kvw.at[1, tile(i), :], kvw.at[2 * side, tile(i), :],
             halo_s.at[side, i], halo_r.at[side, i], patch=left if side else right,
         )
 
-    def project(i):
+    for i in range(3):
         rows = tile(i)
-        x_load(i).wait()
-        xs = x_ref[rows, :].astype(F32)
-        inv = lax.rsqrt(jnp.sum(xs * xs, axis=1, keepdims=True) * (1.0 / D) + 1e-06)
-        h = (xs * inv * gain).astype(BF)
-        hid[rows, :] = h
-        irms[rows, :] = jnp.broadcast_to(inv, (TILE, 128))
-        pr = nt(h, wt[...])
+        pr = nt(hid[rows, :], wt[...])
+        if i < 2:
+            norm(i + 1)
         kvw[1, rows, :] = pr[:, :128].astype(BF)
+        q_raw[rows, :] = pr[:, 128:].astype(BF)
         if i == 0:
             pl.semaphore_wait(barrier, len(near))
-            tell_round(0)
         halo_copy(0, i).start()
         halo_copy(1, i).start()
+    tell_round(0)
+
+    def queries(i, carry):
+        rows = tile(i)
         lane = lax.broadcasted_iota(jnp.int32, (TILE, 128), 1)
-        q = jnp.where(lane < 64, pr[:, 128:].astype(BF).astype(F32), 0.0)
+        q = jnp.where(lane < 64, q_raw[rows, :].astype(F32), 0.0)
         qz[rows, :] = (q * 0.125).astype(BF)
         q_t[:, rows] = jnp.transpose(q)[:64, :].astype(BF)
-
-    for i in range(3):
-        project(i)
+        return carry
+
+    lax.fori_loop(0, 3, queries, 0)
 
     lane12 = lax.broadcasted_iota(jnp.int32, (CAP, 128), 1)
     for load in late_loads:
@@ -220,13 +230,12 @@
             weighted = weighted + fold(e * dp[rows, cols], jnp.sum)
         return total, weighted
 
-    def divide_block(b, q, inv, delta):
+    def divide_block(b, i, q, inv, delta):
         cols = tile(q)
-        for i in range(3):
-            rows = tile(b * 3 + i)
-            att = sc[rows, cols] * inv
-            pt[rows, cols] = att.astype(BF)
-            ds_t[rows, cols] = (att * (dp[rows, cols] - delta)).astype(BF)
+        rows = tile(b * 3 + i)
+        att = sc[rows, cols] * inv
+        pt[rows, cols] = att.astype(BF)
+        ds_t[rows, cols] = (att * (dp[rows, cols] - delta)).astype(BF)
 
     hear_round(0)
     tell_round(1)
@@ -256,25 +265,33 @@
         delta = jnp.sum(weighted, axis=0, keepdims=True) * inv
         scales.append((inv, inv * shrink, delta))
 
-    def near_grad(b):
-        at = tile(b, ROWS)
+    def near_grad(start, size):
+        at = pl.ds(start, size)
         return nn(ds_t[at, :], qz[...]) + nn(pt[at, :], dz[...])
 
-    def grad_copy(side):
+    def grad_copy(side, i):
         return remote(
-            halo_out.at[side], halo_in.at[1 - side], hg_s.at[side], hg_r.at[1 - side],
-            patch=right if side else left,
+            halo_out.at[side, tile(i), :], halo_in.at[1 - side, tile(i), :],
+            hg_s.at[side, i], hg_r.at[1 - side, i], patch=right if side else left,
         )
 
-    for side in range(2):
+    chunks = [(side, i) for i in range(3) for side in range(2)]
+
+    def divide_chunk(b, i, own):
         for q in range(3):
-            divide_block(2 * side, q, scales[q][0], scales[q][2])
-        halo_out[side] = near_grad(2 * side).astype(BF)
-        grad_copy(side).start()
-
-    for q in range(3):
-        divide_block(1, q, scales[q][1], scales[q][2])
-    own_grad[...] = near_grad(1)
+            divide_block(b, i, q, scales[q][own], scales[q][2])
+
+    divide_chunk(0, 0, 0)
+    for n, (side, i) in enumerate(chunks):
+        grads = near_grad((2 * side * 3 + i) * TILE, TILE)
+        if n + 1 < len(chunks):
+            divide_chunk(2 * chunks[n + 1][0], chunks[n + 1][1], 0)
+        halo_out[side, tile(i), :] = grads.astype(BF)
+        grad_copy(side, i).start()
+
+    for i in range(3):
+        divide_chunk(1, i, 1)
+    own_grad[...] = near_grad(ROWS, ROWS)
 
     def query_side(q, carry):
         cols = tile(q)
@@ -367,7 +384,7 @@
 
     lax.fori_loop(0, 3, shares, 0)
 
-    order = [(2, 0), (2, 1), (1, 0), (3, 0), (0, 0), (1, 1), (3, 1), (0, 1)]
+    order = [(2, 0), (1, 0), (3, 0), (2, 1), (1, 1), (3, 1), (0, 0), (0, 1)]
 
     def block_of(o):
         dx, k = order[o]
@@ -377,11 +394,11 @@
     for o in range(8):
         wk[o * 128 : (o + 1) * 128, :] = jnp.transpose(wt[:, tile(block_of(o), 128)].astype(F32)).astype(BF)
 
-    for side in range(2):
-        grad_copy(side).wait_recv()
-
-    def collect(i, carry):
+
+    def collect(i):
         rows = tile(i)
+        for side in range(2):
+            grad_copy(side, i).wait_recv()
         total = (
             own_grad[rows, :] + halo_in[0, rows, :].astype(F32) + halo_in[1, rows, :].astype(F32)
         )
@@ -392,11 +409,10 @@
         prod = prod + jnp.sum(qg, axis=0, keepdims=True)
         for j in range(2):
             m_out[pl.ds(2 * i + j, 1), :] = prod[:, j * 128 : (j + 1) * 128]
-        return carry
 
     m_out[...] = jnp.zeros_like(m_out)
     for i in range(3):
-        collect(i, 0)
+        collect(i)
 
     def core_copy(o):
         return remote(
@@ -410,10 +426,10 @@
             part[o] = some[n * 128 : (n + 1) * 128, :].astype(BF)
             core_copy(o).start()
 
+    part_group(0)
     for n in range(4):
         put(1, n, jnp.transpose(nn(grads_t[0:128, :], hid[:, tile(n)])).astype(BF))
     a_stage(1)
-    part_group(0)
     part_group(1)
     hear_round(2)
 
@@ -428,17 +444,25 @@
         return part[o, tile(core, 64), :].astype(F32) + r1[o].astype(F32)
 
     def chip_copy(o):
-        return remote(
-            s2.at[o], r2.at[o], r2_s.at[o], r2_r.at[o], tensor=block_of(o) * 2 + core
-        )
-
-    for o in range(7):
+        to = (t + 8) % 16 if o == 6 else row0 + (x + order[o][0]) % NX * 2
+        return remote(s2.at[o], r2.at[o], r2_s.at[o], r2_r.at[o], tensor=to)
+
+    def x_sum(k):
+        total = pair_sum(6 + k)
+        for o in range(3 * k, 3 * k + 3):
+            chip_copy(o).wait_recv()
+            total = total + r2[o].astype(F32)
+        return total
+
+    for o in range(6):
         s2[o] = pair_sum(o).astype(BF)
         chip_copy(o).start()
     b_stage(0)
-    feature = pair_sum(7)
     b_stage(1)
+    s2[6] = x_sum(0).astype(BF)
+    chip_copy(6).start()
     z_total(0)
+    feature = x_sum(1)
 
     pltpu.make_async_copy(m_in, m_in, m_r).wait()
     m = m_out[...]
@@ -447,16 +471,15 @@
     m = m * (1.0 / D)
     mean = jnp.concatenate([m[i : i + 1, :] for i in range(6)], axis=1)
 
-    for o in range(7):
-        chip_copy(o).wait_recv()
-        feature = feature + r2[o].astype(F32)
+    chip_copy(6).wait_recv()
+    feature = feature + r2[6].astype(F32)
     og_ref[...] = (ushare[...] + feature * fscale[...] - nshare[...] * mean).astype(BF)
     z_total(1)
 
     for side in range(2):
         for i in range(3):
             halo_copy(side, i).wait_send()
-        grad_copy(side).wait_send()
+            grad_copy(side, i).wait_send()
     for o in range(8):
         core_copy(o).wait_send()
     for o in range(7):
@@ -481,10 +504,7 @@
     dma = pltpu.SemaphoreType.DMA
     grad, proj = pl.pallas_call(
         kernel,
-        out_shape=(
-            jax.ShapeDtypeStruct((64, ROWS), BF),
-            jax.ShapeDtypeStruct((32, 4, 64), F32),
-        ),
+        out_shape=(V((64, ROWS), BF), V((32, 4, 64), F32)),
         in_specs=[hbm] * 8,
         out_specs=(vmem, vmem),
         scratch_shapes=[
@@ -507,6 +527,7 @@
             V((3, ROWS, 128), BF),
             V((3, 128, ROWS), BF),
             V((3, ROWS, 128), BF),
+            V((ROWS, 128), BF),
             V((ROWS, 128), BF),
             V((ROWS, 128), BF),
             V((ROWS, 128), BF),
@@ -534,7 +555,7 @@
             V((7, 64, ROWS), BF),
             dma((3,)), dma, dma((6,)),
             dma((2, 3)), dma((2, 3)),
-            dma((2,)), dma((2,)),
+            dma((2, 3)), dma((2, 3)),
             dma, dma,
             dma((2, 9)), dma((2, 9)),
             dma((2, 3)), dma((2, 3)),

time: 51.9 us -> 46.8 us (0.902)
  Pallas kernels: 48 us -> 44.4 us
  local copies, waits for them, and re-layouts: 3.01 us -> 1.27 us
    pallas_call x1, Pallas kernels: 48 us -> 44.4 us  [per_device(): pl.pallas_call(kernel, out_shape=(V((64, ROWS), BF), V((32, 4, 64), F32))...]
    unnamed x2, local copies, waits for them, and re-layouts: 3.01 us -> 1.27 us
where the time goes in v4:
time: 46.8 us; the launch traced here: 46.3 us
  Pallas kernels  44.4 us (95%)
  local copies, waits for them, and re-layouts  1.27 us (3%)
  between operations  0.64 us (1%)
    pallas_call x1, Pallas kernels, per_device(): pl.pallas_call(kernel, out_shape=(V((64, ROWS), BF), V((32, 4, 64), F32))...  44.4 us
    unnamed x2, local copies, waits for them, and re-layouts  1.27 us

profile of v4, /device:TPU:1, one launch (start us, length us, event | category | flops | bytes accessed | tf_op | source)
XLA Modules:
  0.0 46.3 jit_solution(16205630572408835169)
XLA Ops:
  0.6 44.4 %shard_map.95 = (bf16[64,768]{1,0:T(8,128)(2,1)S(1)}, f32[32,4,64]{2,1,0:T(4,128)S(1)}) custom-call(bf16[768,1024]{1,0:T(8,128)(2,1)} %x_hbm.1, bf16[768,1024]{1,0:T(8,128)(2,1)} %g_hbm.1, f32[1,1024]{1,0:T(1,128)} %bitcast.13, bf16[256,1024]{1,0:T(8,128)(2,1)} %bitcast.10, bf16[256,1024]{1,0:T(8,128)(2,1)} %bitcast.11, s32[32]{0:T(128)} %counts_hbm.1, ...), custom_call_target="tpu_custom_call" | custom-call | flops 4000000000 | bytes 5000000 | tf_op jit(solution)/shard_map/pallas_call | solution.py:505
  45.1 0.6 %copy.12 = bf16[768,64]{0,1:T(8,128)(2,1)} copy(bf16[768,64]{0,1:T(8,128)(2,1)S(1)} %bitcast.9) | data formatting | bytes 196608
  45.7 0.6 %copy.13 = f32[32,4,64]{2,1,0:T(4,128)} copy(f32[32,4,64]{2,1,0:T(4,128)S(1)} %get-tuple-element.7) | data formatting | bytes 65536

commit v5 on v4

--- a/solution.py
+++ b/solution.py
@@ -50,9 +50,9 @@
     x_hbm, g_hbm, gain_hbm, pw_hbm, wn_hbm, counts_hbm, nb_hbm, pv_hbm,
     og_ref, pg_ref,
     x_ref, g_ref, gain_ref, pw_ref, wn_ref, counts_ref, nb_ref, pv_ref, wt, wk, hid, up, irms, fscale, nshare, ushare, kvw, kvt, kaug, qaug, q_raw, qz, dz, q_t,
-    sc, dp, mx, sums, pt, ds_t, halo_out, own_grad, halo_in, att_t, grads_t,
+    sc, dp, tops, sums, pt, ds_t, halo_out, own_grad, halo_in, att_t, grads_t,
     m_out, m_in, pj, a_in, b_out, b_in,
-    part, r1, s2, r2,
+    part, r1, s2, r2, w_acc,
     x_s, g_s, w_s, halo_s, halo_r, hg_s, hg_r, m_s, m_r, a_s, a_r, b_s, b_r,
     c_s, c_r, r2_s, r2_r, known,
 ):
@@ -73,10 +73,12 @@
         pltpu.make_async_copy(pw_hbm, pw_ref, w_s.at[0]),
         pltpu.make_async_copy(wn_hbm, wn_ref, w_s.at[1]),
     ]
+    small_loads = [
+        pltpu.make_async_copy(nb_hbm, nb_ref, w_s.at[3]),
+        pltpu.make_async_copy(pv_hbm, pv_ref, w_s.at[4]),
+    ]
     late_loads = [
         pltpu.make_async_copy(counts_hbm, counts_ref, w_s.at[5]),
-        pltpu.make_async_copy(nb_hbm, nb_ref, w_s.at[3]),
-        pltpu.make_async_copy(pv_hbm, pv_ref, w_s.at[4]),
         pltpu.make_async_copy(g_hbm, g_ref, g_s),
     ]
 
@@ -88,7 +90,7 @@
         load.start()
     for i in range(1, 3):
         x_load(i).start()
-    for load in late_loads:
+    for load in small_loads + late_loads:
         load.start()
 
     barrier = pltpu.get_barrier_semaphore()
@@ -98,23 +100,50 @@
 
     row0 = t - x * 2
     near = [
-        {"patch": left}, {"patch": right}, {"tensor": core_partner},
+        {"tensor": core_partner},
         {"tensor": row0 + (x + 1) % NX * 2}, {"tensor": row0 + (x + 3) % NX * 2},
-        {"tensor": (t + 8) % 16}, patch_of(0, 1), patch_of(1), patch_of(15),
+        {"tensor": (t + 8) % 16}, patch_of(0, 1),
     ]
-    rounds = [near, near + [patch_of(2), patch_of(14)], [near[2], patch_of(4), patch_of(12)]]
+    beside = [patch_of(1), patch_of(15)]
+    far = [[], beside, [near[0], patch_of(2), patch_of(14)], [patch_of(4), patch_of(12)]]
+    has_left, has_right = p > 0, p < 31
+    near_count = 5 + jnp.where(has_left, 1, 0) + jnp.where(has_right, 1, 0)
 
     def tell(semaphore, partners):
         for device in partners:
             pl.semaphore_signal(semaphore, inc=1, device_id=device, device_id_type=MESH)
 
+    def tell_near(semaphore):
+        tell(semaphore, near)
+        for there, other in ((has_left, left), (has_right, right)):
+            pl.when(there)(lambda other=other: tell(semaphore, [{"patch": other}]))
+
     def tell_round(n):
-        tell(known.at[n], rounds[n])
+        if n < 2:
+            tell_near(known.at[n])
+        tell(known.at[n], far[n])
 
     def hear_round(n):
-        pl.semaphore_wait(known.at[n], len(rounds[n]))
-
-    tell(barrier, near)
+        pl.semaphore_wait(known.at[n], len(far[n]) + (near_count if n < 2 else 0))
+
+    tell_near(barrier)
+
+    def if_left(op):
+        pl.when(has_left)(op)
+
+    def if_right(op):
+        pl.when(has_right)(op)
+
+    @pl.when(p == 0)
+    def _():
+        kvw[0] = jnp.zeros((ROWS, 128), BF)
+        halo_in[0] = jnp.zeros((ROWS, 128), BF)
+
+    @pl.when(p == 31)
+    def _():
+        kvw[2] = jnp.zeros((ROWS, 128), BF)
+        halo_in[1] = jnp.zeros((ROWS, 128), BF)
+
 
     def norm(i):
         rows = tile(i)
@@ -143,14 +172,14 @@
     for i in range(3):
         rows = tile(i)
         pr = nt(hid[rows, :], wt[...])
-        if i < 2:
-            norm(i + 1)
         kvw[1, rows, :] = pr[:, :128].astype(BF)
         q_raw[rows, :] = pr[:, 128:].astype(BF)
         if i == 0:
-            pl.semaphore_wait(barrier, len(near))
-        halo_copy(0, i).start()
-        halo_copy(1, i).start()
+            pl.semaphore_wait(barrier, near_count)
+        if_right(halo_copy(0, i).start)
+        if_left(halo_copy(1, i).start)
+        if i < 2:
+            norm(i + 1)
     tell_round(0)
 
     def queries(i, carry):
@@ -164,7 +193,7 @@
     lax.fori_loop(0, 3, queries, 0)
 
     lane12 = lax.broadcasted_iota(jnp.int32, (CAP, 128), 1)
-    for load in late_loads:
+    for load in small_loads:
         load.wait()
     nb = nb_ref[...]
     member = lane12 == 64 + nb[:, 0:1]
@@ -181,19 +210,16 @@
             aux = jnp.where(lane64 == 100, valid[:, s : s + 1], aux)
             kaug[b, s * PIX : (s + 1) * PIX, :] = aux.astype(BF)
 
+    for load in late_loads:
+        load.wait()
     live = counts_ref[p] * PIX
-
-    def upstream(i, carry):
+    for i in range(3):
         rows = tile(i)
         row = lax.broadcasted_iota(jnp.int32, (TILE, 1), 0) + i * TILE
-        g = jnp.where(row < live, g_ref[rows, :].astype(F32), 0.0).astype(BF)
-        up[rows, :] = g
-        og = nt(g, wt[128:256, :])
-        lane = lax.broadcasted_iota(jnp.int32, (TILE, 128), 1)
-        dz[rows, :] = jnp.where(lane >= 64, og, 0.0).astype(BF)
-        return carry
-
-    lax.fori_loop(0, 3, upstream, 0)
+        up[rows, :] = jnp.where(row < live, g_ref[rows, :].astype(F32), 0.0).astype(BF)
+    og = nt(up[...], wt[128:256, :])
+    lane = lax.broadcasted_iota(jnp.int32, (ROWS, 128), 1)
+    dz[...] = jnp.where(lane >= 64, og, 0.0).astype(BF)
     for s in range(CAP):
         rows = slice(s * PIX, (s + 1) * PIX)
         qaug[rows, :] = jnp.where(lane64 < 64, qz[rows, :].astype(F32), member[s : s + 1, :]).astype(BF)
@@ -201,34 +227,33 @@
     def fold(value, op):
         return op(value.reshape(value.shape[0] // 8, 8, value.shape[1]), axis=0)
 
-    def score(b, i):
-        rows = tile(i)
-        at = tile(b * 3 + i)
+    def row(value):
+        return jnp.max(value, axis=0, keepdims=True)
+
+    def soften(b, start, size, group):
+        rows = pl.ds(start, size)
         kv = kvw[b, rows, :].astype(F32)
-        lane = lax.broadcasted_iota(jnp.int32, (TILE, 128), 1)
+        lane = lax.broadcasted_iota(jnp.int32, (size, 128), 1)
         kaug[b, rows, :] = jnp.where(lane < 64, kv, kaug[b, rows, :].astype(F32)).astype(BF)
         kvt[b, :, rows] = jnp.transpose(kv).astype(BF)
         for q in range(3):
             cols = tile(q)
-            s = nt(kaug[b, rows, :], qaug[cols, :])
-            sc[at, cols] = s
-            mx[b * 3 + i, :, cols] = fold(s, jnp.max)
-            dp[at, cols] = nt(kvw[b, rows, :], dz[cols, :])
-
-    def top_of(b, cols):
-        return jnp.max(jnp.max(mx[b * 3 : b * 3 + 3, :, cols], axis=0), axis=0, keepdims=True)
-
-    def raise_block(b, q, top):
-        cols = tile(q)
-        total = jnp.zeros((8, TILE), F32)
-        weighted = jnp.zeros((8, TILE), F32)
-        for i in range(3):
-            rows = tile(b * 3 + i)
-            e = jnp.exp(sc[rows, cols] - top)
-            sc[rows, cols] = e
-            total = total + fold(e, jnp.sum)
-            weighted = weighted + fold(e * dp[rows, cols], jnp.sum)
-        return total, weighted
+            score = nt(kaug[b, rows, :], qaug[cols, :])
+            top = row(fold(score, jnp.max))
+            tops[group, :, cols] = jnp.broadcast_to(top, (8, TILE))
+            total = jnp.zeros((8, TILE), F32)
+            weighted = jnp.zeros((8, TILE), F32)
+            prob_grad = nt(kvw[b, rows, :], dz[cols, :])
+            for i in range(size // TILE):
+                some = slice(i * TILE, (i + 1) * TILE)
+                at = pl.ds(b * ROWS + start + i * TILE, TILE)
+                e = jnp.exp(score[some, :] - top)
+                sc[at, cols] = e
+                dp[at, cols] = prob_grad[some, :]
+                total = total + fold(e, jnp.sum)
+                weighted = weighted + fold(e * prob_grad[some, :], jnp.sum)
+            sums[group, 0, :, cols] = total
+            sums[group, 1, :, cols] = weighted
 
     def divide_block(b, i, q, inv, delta):
         cols = tile(q)
@@ -240,30 +265,30 @@
     hear_round(0)
     tell_round(1)
 
-    for i in range(3):
-        score(1, i)
-    for q in range(3):
-        cols = tile(q)
-        sums[0, :, cols], sums[1, :, cols] = raise_block(1, q, top_of(1, cols))
-
+    soften(1, 0, ROWS, 0)
     for i in range(3):
         for side in range(2):
-            halo_copy(side, i).wait_recv()
-            score(2 * side, i)
-
+            (if_right if side else if_left)(halo_copy(side, i).wait_recv)
+            soften(2 * side, i * TILE, TILE, 1 + 2 * i + side)
+
+    hear_round(1)
+    tell_round(2)
     scales = []
     for q in range(3):
         cols = tile(q)
-        own_top = top_of(1, cols)
-        top = jnp.maximum(own_top, jnp.maximum(top_of(0, cols), top_of(2, cols)))
-        shrink = jnp.exp(own_top - top)
-        total, weighted = sums[0, :, cols] * shrink, sums[1, :, cols] * shrink
-        for b in (0, 2):
-            part_total, part_weighted = raise_block(b, q, top)
-            total, weighted = total + part_total, weighted + part_weighted
+        group_tops = [tops[g, 0:1, cols] for g in range(7)]
+        top = group_tops[0]
+        for other in group_tops[1:]:
+            top = jnp.maximum(top, other)
+        shrink = [jnp.exp(other - top) for other in group_tops]
+        total = jnp.zeros((8, TILE), F32)
+        weighted = jnp.zeros((8, TILE), F32)
+        for g in range(7):
+            total = total + sums[g, 0, :, cols] * shrink[g]
+            weighted = weighted + sums[g, 1, :, cols] * shrink[g]
         inv = 1.0 / jnp.sum(total, axis=0, keepdims=True)
         delta = jnp.sum(weighted, axis=0, keepdims=True) * inv
-        scales.append((inv, inv * shrink, delta))
+        scales.append(([inv * factor for factor in shrink], delta))
 
     def near_grad(start, size):
         at = pl.ds(start, size)
@@ -277,20 +302,21 @@
 
     chunks = [(side, i) for i in range(3) for side in range(2)]
 
-    def divide_chunk(b, i, own):
+    def divide_chunk(b, i):
+        group = 0 if b == 1 else 1 + 2 * i + b // 2
         for q in range(3):
-            divide_block(b, i, q, scales[q][own], scales[q][2])
-
-    divide_chunk(0, 0, 0)
+            divide_block(b, i, q, scales[q][0][group], scales[q][1])
+
+    divide_chunk(0, 0)
     for n, (side, i) in enumerate(chunks):
         grads = near_grad((2 * side * 3 + i) * TILE, TILE)
         if n + 1 < len(chunks):
-            divide_chunk(2 * chunks[n + 1][0], chunks[n + 1][1], 0)
+            divide_chunk(2 * chunks[n + 1][0], chunks[n + 1][1])
         halo_out[side, tile(i), :] = grads.astype(BF)
-        grad_copy(side, i).start()
+        (if_right if side else if_left)(grad_copy(side, i).start)
 
     for i in range(3):
-        divide_chunk(1, i, 1)
+        divide_chunk(1, i)
     own_grad[...] = near_grad(ROWS, ROWS)
 
     def query_side(q, carry):
@@ -361,8 +387,8 @@
             [nn(grads_t[128:192, :], hid[:, cols]), nn(att_t[...], up[:, cols])], axis=0
         )
         put(0, n, jnp.transpose(both).astype(BF))
-    hear_round(1)
-    tell_round(2)
+    hear_round(2)
+    tell_round(3)
     a_stage(0)
 
     odd = core == 1
@@ -398,7 +424,7 @@
     def collect(i):
         rows = tile(i)
         for side in range(2):
-            grad_copy(side, i).wait_recv()
+            (if_left if side else if_right)(grad_copy(side, i).wait_recv)
         total = (
             own_grad[rows, :] + halo_in[0, rows, :].astype(F32) + halo_in[1, rows, :].astype(F32)
         )
@@ -410,10 +436,6 @@
         for j in range(2):
             m_out[pl.ds(2 * i + j, 1), :] = prod[:, j * 128 : (j + 1) * 128]
 
-    m_out[...] = jnp.zeros_like(m_out)
-    for i in range(3):
-        collect(i)
-
     def core_copy(o):
         return remote(
             part.at[o, tile(1 - core, 64), :], r1.at[o], c_s.at[o], c_r.at[o], tensor=core_partner
@@ -426,19 +448,6 @@
             part[o] = some[n * 128 : (n + 1) * 128, :].astype(BF)
             core_copy(o).start()
 
-    part_group(0)
-    for n in range(4):
-        put(1, n, jnp.transpose(nn(grads_t[0:128, :], hid[:, tile(n)])).astype(BF))
-    a_stage(1)
-    part_group(1)
-    hear_round(2)
-
-    def m_send(r, carry):
-        remote(m_out, m_in.at[r - 1], m_s, m_r, tensor=(t + r) % 16).start()
-        return carry
-
-    lax.fori_loop(1, 16, m_send, 0)
-
     def pair_sum(o):
         core_copy(o).wait_recv()
         return part[o, tile(core, 64), :].astype(F32) + r1[o].astype(F32)
@@ -446,6 +455,10 @@
     def chip_copy(o):
         to = (t + 8) % 16 if o == 6 else row0 + (x + order[o][0]) % NX * 2
         return remote(s2.at[o], r2.at[o], r2_s.at[o], r2_r.at[o], tensor=to)
+
+    def x_send(o):
+        s2[o] = pair_sum(o).astype(BF)
+        chip_copy(o).start()
 
     def x_sum(k):
         total = pair_sum(6 + k)
@@ -454,14 +467,37 @@
             total = total + r2[o].astype(F32)
         return total
 
-    for o in range(6):
-        s2[o] = pair_sum(o).astype(BF)
-        chip_copy(o).start()
+    m_out[...] = jnp.zeros_like(m_out)
+    for i in range(2):
+        collect(i)
+    for n in range(4):
+        cols = tile(n)
+        w_acc[:, cols] = nn(grads_t[0:128, 0:512], hid[0:512, cols])
+    collect(2)
+    part_group(0)
+    for n in range(4):
+        cols = tile(n)
+        total = w_acc[:, cols] + nn(grads_t[0:128, 512:768], hid[512:768, cols])
+        put(1, n, jnp.transpose(total).astype(BF))
+    a_stage(1)
+    for o in range(3):
+        x_send(o)
+    part_group(1)
+
+    def m_send(r, carry):
+        remote(m_out, m_in.at[r - 1], m_s, m_r, tensor=(t + r) % 16).start()
+        return carry
+
+    lax.fori_loop(1, 16, m_send, 0)
+
+    hear_round(3)
     b_stage(0)
+    for o in (1, 2, 0):
+        chip_copy(o).wait_send()
+        x_send(o + 3)
     b_stage(1)
     s2[6] = x_sum(0).astype(BF)
     chip_copy(6).start()
-    z_total(0)
     feature = x_sum(1)
 
     pltpu.make_async_copy(m_in, m_in, m_r).wait()
@@ -474,15 +510,16 @@
     chip_copy(6).wait_recv()
     feature = feature + r2[6].astype(F32)
     og_ref[...] = (ushare[...] + feature * fscale[...] - nshare[...] * mean).astype(BF)
+    z_total(0)
     z_total(1)
 
     for side in range(2):
         for i in range(3):
-            halo_copy(side, i).wait_send()
-            grad_copy(side, i).wait_send()
+            (if_left if side else if_right)(halo_copy(side, i).wait_send)
+            (if_right if side else if_left)(grad_copy(side, i).wait_send)
     for o in range(8):
         core_copy(o).wait_send()
-    for o in range(7):
+    for o in range(3, 7):
         chip_copy(o).wait_send()
     for h in range(2):
         for n in range(9):
@@ -534,8 +571,8 @@
             V((64, ROWS), BF),
             V((3 * ROWS, ROWS), F32),
             V((3 * ROWS, ROWS), F32),
-            V((9, 8, ROWS), F32),
-            V((2, 8, ROWS), F32),
+            V((7, 8, ROWS), F32),
+            V((7, 2, 8, ROWS), F32),
             V((3 * ROWS, ROWS), BF),
             V((3 * ROWS, ROWS), BF),
             V((2, ROWS, 128), BF),
@@ -553,6 +590,7 @@
             V((8, 64, ROWS), BF),
             V((7, 64, ROWS), BF),
             V((7, 64, ROWS), BF),
+            V((128, D), F32),
             dma((3,)), dma, dma((6,)),
             dma((2, 3)), dma((2, 3)),
             dma((2, 3)), dma((2, 3)),
@@ -561,7 +599,7 @@
             dma((2, 3)), dma((2, 3)),
             dma((8,)), dma((8,)),
             dma((7,)), dma((7,)),
-            pltpu.SemaphoreType.REGULAR((3,)),
+            pltpu.SemaphoreType.REGULAR((4,)),
         ],
         compiler_params=pltpu.CompilerParams(
             collective_id=0, has_side_effects=True, vmem_limit_bytes=56 * 1024 * 1024

time: 46.8 us -> 46.5 us (level)
  the two profiles are of different devices: /device:TPU:1 before, /device:TPU:8 now
where the time goes in v5:
time: 46.5 us; the launch traced here: 46.4 us
  Pallas kernels  44.5 us (96%)
  local copies, waits for them, and re-layouts  1.27 us (3%)
  between operations  0.64 us (1%)
    pallas_call x1, Pallas kernels, per_device(): pl.pallas_call(kernel, out_shape=(V((64, ROWS), BF), V((32, 4, 64), F32))...  44.5 us
    unnamed x2, local copies, waits for them, and re-layouts  1.27 us

profile of v5, /device:TPU:8, one launch (start us, length us, event | category | flops | bytes accessed | tf_op | source)
XLA Modules:
  0.0 46.4 jit_solution(9805401471404867803)
XLA Ops:
  0.6 44.5 %shard_map.95 = (bf16[64,768]{1,0:T(8,128)(2,1)S(1)}, f32[32,4,64]{2,1,0:T(4,128)S(1)}) custom-call(bf16[768,1024]{1,0:T(8,128)(2,1)} %x_hbm.1, bf16[768,1024]{1,0:T(8,128)(2,1)} %g_hbm.1, f32[1,1024]{1,0:T(1,128)} %bitcast.13, bf16[256,1024]{1,0:T(8,128)(2,1)} %bitcast.10, bf16[256,1024]{1,0:T(8,128)(2,1)} %bitcast.11, s32[32]{0:T(128)} %counts_hbm.1, ...), custom_call_target="tpu_custom_call" | custom-call | flops 4000000000 | bytes 5000000 | tf_op jit(solution)/shard_map/pallas_call | solution.py:542
  45.1 0.6 %copy.12 = bf16[768,64]{0,1:T(8,128)(2,1)} copy(bf16[768,64]{0,1:T(8,128)(2,1)S(1)} %bitcast.9) | data formatting | bytes 196608
  45.7 0.6 %copy.13 = f32[32,4,64]{2,1,0:T(4,128)} copy(f32[32,4,64]{2,1,0:T(4,128)S(1)} %get-tuple-element.7) | data formatting | bytes 65536
